TPU v7x, 32 devices: a whole 2x2x4 slice. The times are simulated.
32 devices in a mesh: dp: 4 (over z), pipe: 4 (over x, core), tensor: 2 (over y).
Axes of the slice: x: 2, y: 2, z: 4, core: 2. Of those that a mesh axis runs over, the one named last changes fastest.
Arguments:
- inputs: bfloat16 [2, 512, 8192], P(None, 'dp', 'tensor'), may hold values from -6 to 6
- cotangent: bfloat16 [2, 512, 8192], P(None, 'dp', 'tensor'), may hold values from -0.19921875 to 0.19921875
- up_weight: bfloat16 [4, 32, 6, 256, 256], P('pipe', 'tensor'), may hold values from -0.15625 to 0.15625
- down_weight: bfloat16 [4, 32, 6, 256, 256], P('pipe', 'tensor'), may hold values from -0.15625 to 0.15625
Outputs:
- up_grad: float32 [4, 32, 6, 256, 256], P('pipe', 'tensor')
- down_grad: float32 [4, 32, 6, 256, 256], P('pipe', 'tensor')
All inputs are finite; a program needn't handle non-finite values.
Results may differ from a plain program's by a relative error of at most 0.02.
Values may be sent and summed in bfloat16 or wider, within the bound.
A program may use at most 192 MiB of HBM per device.

v0:
```python
import jax
import jax.numpy as jnp
import numpy as np
from jax import lax
from jax.sharding import PartitionSpec as P

ROOT_HALF = 0.7071067811865476
INV_ROOT_TWO_PI = 0.3989422804014327


def swapped(block, axis, distance):
    count = lax.axis_size(axis)
    route = []
    for low in range(count):
        high = low | 1 << distance
        if high != low and high < count:
            route += [(low, high), (high, low)]
    return lax.ppermute(block, axis, route)


def passed_along(x, axis, by):
    size = lax.axis_size(axis)
    pairs = [(i, i + by) for i in range(size) if 0 <= i + by < size]
    return lax.ppermute(x, axis, pairs)


def offsets_table(count):
    return [0] + [2**j for j in range(count - 1)]


def gelu_value(v):
    return v * 0.5 * (1.0 + lax.erf(v * ROOT_HALF))


def gelu_slope(v):
    return 0.5 * (1.0 + lax.erf(v * ROOT_HALF)) + v * INV_ROOT_TWO_PI * jnp.exp(-0.5 * v * v)


def local_flip(values, shift_by, axis_pos):
    if shift_by == 0:
        return values
    width = values.shape[axis_pos]
    return jnp.take(
        values, np.array([j ^ shift_by for j in range(width)], dtype=np.int32), axis=axis_pos
    )


def forward_sender(values, bit_pos):
    return swapped(values, "tensor", bit_pos)


def partner_stack(values, count, sender):
    width = values.shape[1]
    stacked = []
    for s in offsets_table(count):
        if s < width:
            stacked.append(local_flip(values, s, 1))
        else:
            stacked.append(sender(values, (s // width).bit_length() - 1))
    return jnp.stack(stacked, axis=2)


def paired_stack(first, second, count):
    width = first.shape[1]
    first_list, second_list = ([], [])
    for s in offsets_table(count):
        if s < width:
            first_list.append(local_flip(first, s, 1))
            second_list.append(local_flip(second, s, 1))
        else:
            moved_first, moved_second = swapped(
                (first, second), "tensor", (s // width).bit_length() - 1
            )
            first_list.append(moved_first)
            second_list.append(moved_second)
    return (jnp.stack(first_list, axis=2), jnp.stack(second_list, axis=2))


def transpose_apply(grads, weight):
    count = weight.shape[1]
    width = weight.shape[0]
    terms = jnp.einsum("tlc,lkbc->tlkb", grads, weight, preferred_element_type=jnp.float32)
    summed = jnp.zeros(grads.shape, jnp.float32)
    for k, s in enumerate(offsets_table(count)):
        if s < width:
            summed = summed + local_flip(terms[:, :, k], s, 1)
        else:
            summed = summed + swapped(terms[:, :, k], "tensor", (s // width).bit_length() - 1)
    return summed


def store_slot(buffer, index, fresh, active):
    old_value = lax.dynamic_index_in_dim(buffer, index, 0, keepdims=False)
    return lax.dynamic_update_index_in_dim(buffer, jnp.where(active, fresh, old_value), index, 0)


def read_slot(buffer, index):
    return lax.dynamic_index_in_dim(buffer, index, 0, keepdims=False)


def per_device(inputs, cotangent, up_weight, down_weight):
    w_up = up_weight[0]
    w_down = down_weight[0]
    blocks_dev, count, block_size = (w_up.shape[0], w_up.shape[1], w_up.shape[2])
    micro, tok_rows = (inputs.shape[0], inputs.shape[1])
    segment = lax.axis_index("pipe")
    sections = lax.axis_size("pipe")
    steps_total = micro + sections - 1
    block_shape = (micro, tok_rows, blocks_dev, block_size)
    saved = (
        jnp.zeros(block_shape, jnp.bfloat16),
        jnp.zeros(block_shape, jnp.float32),
        jnp.zeros(block_shape, jnp.bfloat16),
    )

    def forward_step(moment, carry):
        outgoing, held = carry
        received = passed_along(outgoing, "pipe", 1)
        index = moment - segment
        active = jnp.logical_and(index >= 0, index < micro)
        index = jnp.clip(index, 0, micro - 1)
        own_rows = lax.dynamic_index_in_dim(inputs, index, 0, keepdims=False)
        layer_in = jnp.where(segment == 0, own_rows, received).reshape(
            tok_rows, blocks_dev, block_size
        )
        in_stack = partner_stack(layer_in, count, forward_sender)
        hidden = jnp.einsum("tlkb,lkbc->tlc", in_stack, w_up, preferred_element_type=jnp.float32)
        act = gelu_value(hidden).astype(jnp.bfloat16)
        act_stack = partner_stack(act, count, forward_sender)
        mixed = jnp.einsum("tlkb,lkbc->tlc", act_stack, w_down, preferred_element_type=jnp.float32)
        layer_out = (layer_in.astype(jnp.float32) + mixed).astype(jnp.bfloat16)
        fresh = (layer_in, hidden, act) + ()
        held = tuple(
            (store_slot(buf, index, new_value, active) for buf, new_value in zip(held, fresh))
        )
        return (layer_out.reshape(tok_rows, blocks_dev * block_size), held)

    start_out = jnp.zeros((tok_rows, blocks_dev * block_size), jnp.bfloat16)
    last_out, saved = lax.fori_loop(0, steps_total, forward_step, (start_out, saved))

    def backward_step(moment, carry):
        outgoing, grad_up, grad_down = carry
        received = passed_along(outgoing, "pipe", -1)
        index = moment - (sections - 1 - segment)
        active = jnp.logical_and(index >= 0, index < micro)
        index = jnp.clip(index, 0, micro - 1)
        own_rows = lax.dynamic_index_in_dim(cotangent, index, 0, keepdims=False)
        grads = jnp.where(segment == sections - 1, own_rows, received).reshape(
            tok_rows, blocks_dev, block_size
        )
        layer_in = read_slot(saved[0], index)
        hidden = read_slot(saved[1], index)
        act = read_slot(saved[2], index)
        in_stack, act_stack = paired_stack(layer_in, act, count)
        grad_act = transpose_apply(grads, w_down)
        grad_hidden = (grad_act * gelu_slope(hidden)).astype(jnp.bfloat16)
        grad_in = (grads.astype(jnp.float32) + transpose_apply(grad_hidden, w_up)).astype(
            jnp.bfloat16
        )
        down_term = jnp.einsum(
            "tlkb,tlc->lkbc", act_stack, grads, preferred_element_type=jnp.float32
        )
        up_term = jnp.einsum(
            "tlkb,tlc->lkbc", in_stack, grad_hidden, preferred_element_type=jnp.float32
        )
        grad_down = grad_down + jnp.where(active, down_term, 0.0)
        grad_up = grad_up + jnp.where(active, up_term, 0.0)
        return (grad_in.reshape(tok_rows, blocks_dev * block_size), grad_up, grad_down)

    empty_grad = jnp.zeros((blocks_dev, count, block_size, block_size), jnp.float32)
    first_out, grad_up, grad_down = lax.fori_loop(
        0, steps_total, backward_step, (start_out, empty_grad, empty_grad)
    )
    grad_up, grad_down = lax.psum((grad_up, grad_down), "dp")
    return (grad_up[None], grad_down[None])


def solution(mesh):
    in_specs = (
        P(None, "dp", "tensor"),
        P(None, "dp", "tensor"),
        P("pipe", "tensor", None, None, None),
        P("pipe", "tensor", None, None, None),
    )
    out_specs = (P("pipe", "tensor", None, None, None), P("pipe", "tensor", None, None, None))
    return jax.shard_map(
        per_device, mesh=mesh, in_specs=in_specs, out_specs=out_specs, check_vma=False
    )
```

profile of v0, /device:TPU:1, one launch (start us, length us, event | category | flops | bytes accessed | tf_op | source)
XLA Modules:
  0.0 3230.7 jit_solution(15646085986640376864)
XLA Ops:
  24.9 409.8 %while.44 = (s32[]{:T(128)}, bf16[128,4096]{0,1:T(8,128)(2,1)}, bf16[2,128,16,256]{1,3,2,0:T(8,128)(2,1)}, f32[2,128,16,256]{3,1,2,0:T(8,128)}, bf16[2,128,16,25...) while((s32[]{:T(128)}, bf16[128,4096]{0,1:T(8,128)(2,1)}, ...), condition=%wide.region_1.3_spmd.clone.clone, body=%wide.region_0.2_spmd.sunk.clone.clone.sunk | while | flops 3227521024 | bytes 191907184 | solution.py:139
  435.8 1102.4 %while.45 = (s32[]{:T(128)}, bf16[128,4096]{0,1:T(8,128)(2,1)}, f32[16,6,256,256]{3,2,1,0:T(8,128)}, f32[16,6,256,256]{3,2,1,0:T(8,128)}, pred[]{:T(512)}, /*ind...) while((s32[]{:T(128)}, bf16[128,4096]{0,1:T(8,128)(2,1)}, ...), condition=%wide.region_3.6_spmd.clone.clone.clone, body=%wide.region_2.5_spmd.sunk.clone.clone.clone.sunk | while | flops 6492786688 | bytes 387991424 | solution.py:171
  477.1 13.3 convolution_bitcast_fusion.4
  533.1 25.7 collective-permute-done.4
  613.6 31.6 collective-permute-done.5
  693.5 13.3 convolution_bitcast_fusion.4
  736.8 20.7 select_add_fusion.5
  757.5 19.7 collective-permute-done.4
  819.4 20.7 select_add_fusion.4
  840.2 25.5 collective-permute-done.5
  958.2 20.7 select_add_fusion.5
  978.9 20.6 collective-permute-done.4
  1041.5 20.7 select_add_fusion.4
  1062.2 24.9 collective-permute-done.5
  1180.2 20.7 select_add_fusion.5
  1200.9 20.6 collective-permute-done.4
  1263.5 20.7 select_add_fusion.4
  1284.2 24.9 collective-permute-done.5
  1402.3 20.7 select_add_fusion.5
  1423.0 20.6 collective-permute-done.4
  1485.5 20.7 select_add_fusion.4
  1506.3 24.9 collective-permute-done.5
  1538.2 1652.6 %all-reduce.3.cloned.1.call-done = (f32[1,16,6,256,256]{4,3,2,1,0:T(8,128)}, f32[1,16,6,256,256]{4,3,2,1,0:T(8,128)}) async-done(((f32[1,16,6,256,256]{4,3,2,1,0:T(8,128)}, f32[1,16,6,256,256]{4,3,2,1,0:T(8,128)}), (f32[1,16,6,256,256]{4,3,2,1,0:T(8,128)}, f32[1,16,6,256,256]{4,3,2,1,0:T(8,128)})) %all-reduce.3.cloned.1.call-update) | async-done | bytes 50331664 | tf_op jit(solution)/shard_map/psum | solution.py:174
  3190.8 18.3 copy.179
  (631 shorter events, 1112.5 us)
Async XLA Ops:
  7.2 3183.6 %all-reduce.3.cloned.1.call-start = ((), (), s32[]{:S(2)}) async-start(), calls=%async_computation | async-start | bytes 100663296 | tf_op jit(solution)/shard_map/psum | solution.py:174
  437.8 77.8 %collective-permute-start.7 = (bf16[128,16,256]{0,2,1:T(8,128)(2,1)S(1)}, bf16[128,16,256]{0,2,1:T(8,128)(2,1)}, u32[]{:S(2)}, u32[]{:S(2)}) collective-permute-start(bf16[128,16,256]{0,2,1:T(8,128)(2,1)S(1)} %bitcast.394), channel_id=1, source_target_pairs={{0,1},{1,0},{2,3},{3,2},{4,5},{5,4},{6,7},{7,6},{8,9},{9,8},{10,11... | collective-permute-start | bytes 3145736 | tf_op jit(solution)/shard_map/while/body/eval_jaxpr/ppermute | solution.py:18
  440.9 77.1 %collective-permute-start.6 = (bf16[128,16,256]{0,2,1:T(8,128)(2,1)S(1)}, bf16[128,16,256]{0,2,1:T(8,128)(2,1)}, u32[]{:S(2)}, u32[]{:S(2)}) collective-permute-start(bf16[128,16,256]{0,2,1:T(8,128)(2,1)S(1)} %dynamic-slice_bitcast_fusion.2), channel_id=1, source_target_pairs={{0,1},{1,0},{2,3},{3,2},{4,5},{5,4},{6,7},{7,6},{8,9},{9,8},{10,11... | collective-permute-start | bytes 3145736 | tf_op jit(solution)/shard_map/while/body/eval_jaxpr/ppermute | solution.py:18
  514.2 44.6 %collective-permute-start.4 = (f32[128,16,256]{2,0,1:T(8,128)}, f32[128,16,256]{2,0,1:T(8,128)}, u32[]{:S(2)}, u32[]{:S(2)}) collective-permute-start(f32[128,16,256]{2,0,1:T(8,128)} %get-tuple-element.1482), channel_id=1, source_target_pairs={{0,1},{1,0},{2,3},{3,2},{4,5},{5,4},{6,7},{7,6},{8,9},{9,8},{10,11... | collective-permute-start | bytes 6291464 | tf_op jit(solution)/shard_map/while/body/eval_jaxpr/ppermute | solution.py:18
  599.3 45.9 %collective-permute-start.5 = (f32[128,16,256]{2,0,1:T(8,128)}, f32[128,16,256]{2,0,1:T(8,128)}, u32[]{:S(2)}, u32[]{:S(2)}) collective-permute-start(f32[128,16,256]{2,0,1:T(8,128)} %get-tuple-element.1491), channel_id=1, source_target_pairs={{0,1},{1,0},{2,3},{3,2},{4,5},{5,4},{6,7},{7,6},{8,9},{9,8},{10,11... | collective-permute-start | bytes 6291464 | tf_op jit(solution)/shard_map/while/body/eval_jaxpr/ppermute | solution.py:18
  654.1 77.8 %collective-permute-start.7 = (bf16[128,16,256]{0,2,1:T(8,128)(2,1)S(1)}, bf16[128,16,256]{0,2,1:T(8,128)(2,1)}, u32[]{:S(2)}, u32[]{:S(2)}) collective-permute-start(bf16[128,16,256]{0,2,1:T(8,128)(2,1)S(1)} %bitcast.394), channel_id=1, source_target_pairs={{0,1},{1,0},{2,3},{3,2},{4,5},{5,4},{6,7},{7,6},{8,9},{9,8},{10,11... | collective-permute-start | bytes 3145736 | tf_op jit(solution)/shard_map/while/body/eval_jaxpr/ppermute | solution.py:18
  657.2 77.2 %collective-permute-start.6 = (bf16[128,16,256]{0,2,1:T(8,128)(2,1)S(1)}, bf16[128,16,256]{0,2,1:T(8,128)(2,1)}, u32[]{:S(2)}, u32[]{:S(2)}) collective-permute-start(bf16[128,16,256]{0,2,1:T(8,128)(2,1)S(1)} %dynamic-slice_bitcast_fusion.2), channel_id=1, source_target_pairs={{0,1},{1,0},{2,3},{3,2},{4,5},{5,4},{6,7},{7,6},{8,9},{9,8},{10,11... | collective-permute-start | bytes 3145736 | tf_op jit(solution)/shard_map/while/body/eval_jaxpr/ppermute | solution.py:18
  730.5 46.7 %collective-permute-start.4 = (f32[128,16,256]{2,0,1:T(8,128)}, f32[128,16,256]{2,0,1:T(8,128)}, u32[]{:S(2)}, u32[]{:S(2)}) collective-permute-start(f32[128,16,256]{2,0,1:T(8,128)} %get-tuple-element.1482), channel_id=1, source_target_pairs={{0,1},{1,0},{2,3},{3,2},{4,5},{5,4},{6,7},{7,6},{8,9},{9,8},{10,11... | collective-permute-start | bytes 6291464 | tf_op jit(solution)/shard_map/while/body/eval_jaxpr/ppermute | solution.py:18
  817.7 48.0 %collective-permute-start.5 = (f32[128,16,256]{2,0,1:T(8,128)}, f32[128,16,256]{2,0,1:T(8,128)}, u32[]{:S(2)}, u32[]{:S(2)}) collective-permute-start(f32[128,16,256]{2,0,1:T(8,128)} %get-tuple-element.1491), channel_id=1, source_target_pairs={{0,1},{1,0},{2,3},{3,2},{4,5},{5,4},{6,7},{7,6},{8,9},{9,8},{10,11... | collective-permute-start | bytes 6291464 | tf_op jit(solution)/shard_map/while/body/eval_jaxpr/ppermute | solution.py:18
  874.6 78.7 %collective-permute-start.7 = (bf16[128,16,256]{0,2,1:T(8,128)(2,1)S(1)}, bf16[128,16,256]{0,2,1:T(8,128)(2,1)}, u32[]{:S(2)}, u32[]{:S(2)}) collective-permute-start(bf16[128,16,256]{0,2,1:T(8,128)(2,1)S(1)} %bitcast.394), channel_id=1, source_target_pairs={{0,1},{1,0},{2,3},{3,2},{4,5},{5,4},{6,7},{7,6},{8,9},{9,8},{10,11... | collective-permute-start | bytes 3145736 | tf_op jit(solution)/shard_map/while/body/eval_jaxpr/ppermute | solution.py:18
  877.2 78.5 %collective-permute-start.6 = (bf16[128,16,256]{0,2,1:T(8,128)(2,1)S(1)}, bf16[128,16,256]{0,2,1:T(8,128)(2,1)}, u32[]{:S(2)}, u32[]{:S(2)}) collective-permute-start(bf16[128,16,256]{0,2,1:T(8,128)(2,1)S(1)} %dynamic-slice_bitcast_fusion.2), channel_id=1, source_target_pairs={{0,1},{1,0},{2,3},{3,2},{4,5},{5,4},{6,7},{7,6},{8,9},{9,8},{10,11... | collective-permute-start | bytes 3145736 | tf_op jit(solution)/shard_map/while/body/eval_jaxpr/ppermute | solution.py:18
  877.5 35.9 %collective-permute-start.3 = (bf16[128,4096]{0,1:T(8,128)(2,1)}, bf16[128,4096]{0,1:T(8,128)(2,1)}, u32[]{:S(2)}, u32[]{:S(2)}) collective-permute-start(bf16[128,4096]{0,1:T(8,128)(2,1)} %get-tuple-element.1567), channel_id=1, source_target_pairs={{2,0},{4,2},{6,4},{3,1},{5,3},{7,5},{10,8},{12,10},{14,12},{11,9},... | collective-permute-start | bytes 3145736 | tf_op jit(solution)/shard_map/while/body/eval_jaxpr/ppermute | solution.py:24
  951.9 47.6 %collective-permute-start.4 = (f32[128,16,256]{2,0,1:T(8,128)}, f32[128,16,256]{2,0,1:T(8,128)}, u32[]{:S(2)}, u32[]{:S(2)}) collective-permute-start(f32[128,16,256]{2,0,1:T(8,128)} %get-tuple-element.1482), channel_id=1, source_target_pairs={{0,1},{1,0},{2,3},{3,2},{4,5},{5,4},{6,7},{7,6},{8,9},{9,8},{10,11... | collective-permute-start | bytes 6291464 | tf_op jit(solution)/shard_map/while/body/eval_jaxpr/ppermute | solution.py:18
  1040.0 47.1 %collective-permute-start.5 = (f32[128,16,256]{2,0,1:T(8,128)}, f32[128,16,256]{2,0,1:T(8,128)}, u32[]{:S(2)}, u32[]{:S(2)}) collective-permute-start(f32[128,16,256]{2,0,1:T(8,128)} %get-tuple-element.1491), channel_id=1, source_target_pairs={{0,1},{1,0},{2,3},{3,2},{4,5},{5,4},{6,7},{7,6},{8,9},{9,8},{10,11... | collective-permute-start | bytes 6291464 | tf_op jit(solution)/shard_map/while/body/eval_jaxpr/ppermute | solution.py:18
  1096.0 79.3 %collective-permute-start.7 = (bf16[128,16,256]{0,2,1:T(8,128)(2,1)S(1)}, bf16[128,16,256]{0,2,1:T(8,128)(2,1)}, u32[]{:S(2)}, u32[]{:S(2)}) collective-permute-start(bf16[128,16,256]{0,2,1:T(8,128)(2,1)S(1)} %bitcast.394), channel_id=1, source_target_pairs={{0,1},{1,0},{2,3},{3,2},{4,5},{5,4},{6,7},{7,6},{8,9},{9,8},{10,11... | collective-permute-start | bytes 3145736 | tf_op jit(solution)/shard_map/while/body/eval_jaxpr/ppermute | solution.py:18
  1098.9 78.9 %collective-permute-start.6 = (bf16[128,16,256]{0,2,1:T(8,128)(2,1)S(1)}, bf16[128,16,256]{0,2,1:T(8,128)(2,1)}, u32[]{:S(2)}, u32[]{:S(2)}) collective-permute-start(bf16[128,16,256]{0,2,1:T(8,128)(2,1)S(1)} %dynamic-slice_bitcast_fusion.2), channel_id=1, source_target_pairs={{0,1},{1,0},{2,3},{3,2},{4,5},{5,4},{6,7},{7,6},{8,9},{9,8},{10,11... | collective-permute-start | bytes 3145736 | tf_op jit(solution)/shard_map/while/body/eval_jaxpr/ppermute | solution.py:18
  1099.0 36.5 %collective-permute-start.3 = (bf16[128,4096]{0,1:T(8,128)(2,1)}, bf16[128,4096]{0,1:T(8,128)(2,1)}, u32[]{:S(2)}, u32[]{:S(2)}) collective-permute-start(bf16[128,4096]{0,1:T(8,128)(2,1)} %get-tuple-element.1567), channel_id=1, source_target_pairs={{2,0},{4,2},{6,4},{3,1},{5,3},{7,5},{10,8},{12,10},{14,12},{11,9},... | collective-permute-start | bytes 3145736 | tf_op jit(solution)/shard_map/while/body/eval_jaxpr/ppermute | solution.py:24
  1173.9 47.6 %collective-permute-start.4 = (f32[128,16,256]{2,0,1:T(8,128)}, f32[128,16,256]{2,0,1:T(8,128)}, u32[]{:S(2)}, u32[]{:S(2)}) collective-permute-start(f32[128,16,256]{2,0,1:T(8,128)} %get-tuple-element.1482), channel_id=1, source_target_pairs={{0,1},{1,0},{2,3},{3,2},{4,5},{5,4},{6,7},{7,6},{8,9},{9,8},{10,11... | collective-permute-start | bytes 6291464 | tf_op jit(solution)/shard_map/while/body/eval_jaxpr/ppermute | solution.py:18
  1262.0 47.1 %collective-permute-start.5 = (f32[128,16,256]{2,0,1:T(8,128)}, f32[128,16,256]{2,0,1:T(8,128)}, u32[]{:S(2)}, u32[]{:S(2)}) collective-permute-start(f32[128,16,256]{2,0,1:T(8,128)} %get-tuple-element.1491), channel_id=1, source_target_pairs={{0,1},{1,0},{2,3},{3,2},{4,5},{5,4},{6,7},{7,6},{8,9},{9,8},{10,11... | collective-permute-start | bytes 6291464 | tf_op jit(solution)/shard_map/while/body/eval_jaxpr/ppermute | solution.py:18
  1318.1 79.3 %collective-permute-start.7 = (bf16[128,16,256]{0,2,1:T(8,128)(2,1)S(1)}, bf16[128,16,256]{0,2,1:T(8,128)(2,1)}, u32[]{:S(2)}, u32[]{:S(2)}) collective-permute-start(bf16[128,16,256]{0,2,1:T(8,128)(2,1)S(1)} %bitcast.394), channel_id=1, source_target_pairs={{0,1},{1,0},{2,3},{3,2},{4,5},{5,4},{6,7},{7,6},{8,9},{9,8},{10,11... | collective-permute-start | bytes 3145736 | tf_op jit(solution)/shard_map/while/body/eval_jaxpr/ppermute | solution.py:18
  1320.9 78.9 %collective-permute-start.6 = (bf16[128,16,256]{0,2,1:T(8,128)(2,1)S(1)}, bf16[128,16,256]{0,2,1:T(8,128)(2,1)}, u32[]{:S(2)}, u32[]{:S(2)}) collective-permute-start(bf16[128,16,256]{0,2,1:T(8,128)(2,1)S(1)} %dynamic-slice_bitcast_fusion.2), channel_id=1, source_target_pairs={{0,1},{1,0},{2,3},{3,2},{4,5},{5,4},{6,7},{7,6},{8,9},{9,8},{10,11... | collective-permute-start | bytes 3145736 | tf_op jit(solution)/shard_map/while/body/eval_jaxpr/ppermute | solution.py:18
  1321.0 36.5 %collective-permute-start.3 = (bf16[128,4096]{0,1:T(8,128)(2,1)}, bf16[128,4096]{0,1:T(8,128)(2,1)}, u32[]{:S(2)}, u32[]{:S(2)}) collective-permute-start(bf16[128,4096]{0,1:T(8,128)(2,1)} %get-tuple-element.1567), channel_id=1, source_target_pairs={{2,0},{4,2},{6,4},{3,1},{5,3},{7,5},{10,8},{12,10},{14,12},{11,9},... | collective-permute-start | bytes 3145736 | tf_op jit(solution)/shard_map/while/body/eval_jaxpr/ppermute | solution.py:24
  1396.0 47.6 %collective-permute-start.4 = (f32[128,16,256]{2,0,1:T(8,128)}, f32[128,16,256]{2,0,1:T(8,128)}, u32[]{:S(2)}, u32[]{:S(2)}) collective-permute-start(f32[128,16,256]{2,0,1:T(8,128)} %get-tuple-element.1482), channel_id=1, source_target_pairs={{0,1},{1,0},{2,3},{3,2},{4,5},{5,4},{6,7},{7,6},{8,9},{9,8},{10,11... | collective-permute-start | bytes 6291464 | tf_op jit(solution)/shard_map/while/body/eval_jaxpr/ppermute | solution.py:18
  1484.1 47.1 %collective-permute-start.5 = (f32[128,16,256]{2,0,1:T(8,128)}, f32[128,16,256]{2,0,1:T(8,128)}, u32[]{:S(2)}, u32[]{:S(2)}) collective-permute-start(f32[128,16,256]{2,0,1:T(8,128)} %get-tuple-element.1491), channel_id=1, source_target_pairs={{0,1},{1,0},{2,3},{3,2},{4,5},{5,4},{6,7},{7,6},{8,9},{9,8},{10,11... | collective-permute-start | bytes 6291464 | tf_op jit(solution)/shard_map/while/body/eval_jaxpr/ppermute | solution.py:18
  (97 other events, 782.8 us)
Sparse Core Ops, SparseCore 0:
  1538.3 1652.4 all-reduce.2
where the time goes:
time: 3240 us; the launch traced here: 3230 us
  waiting for transfers between devices  1990 us (61%)
  local copies, waits for them, and re-layouts  672 us (21%)
  matrix products  406 us (13%)
  other arithmetic  81.5 us (3%)
  starting transfers between devices  67.4 us (2%)
    psum x1, waiting for transfers between devices, per_device(): grad_up, grad_down = lax.psum((grad_up, grad_down), 'dp')  1650 us
    ppermute x30, waiting for transfers between devices, swapped(): return lax.ppermute(block, axis, route)  307 us
    gather x120, local copies, waits for them, and re-layouts, local_flip(): jnp.take(values, np.array([j ^ shift_by for j in range(width)], dtype=np....  255 us
    while x250, local copies, waits for them, and re-layouts  142 us
    dot_general x10, matrix products, transpose_apply(): jnp.einsum('tlc,lkbc->tlkb', grads, weight, preferred_element_type=jnp.fl...  133 us
    dot_general x5, matrix products, backward_step(): jnp.einsum('tlkb,tlc->lkbc', in_stack, grad_hidden, preferred_element_typ...  95.6 us
    dot_general x5, matrix products, backward_step(): jnp.einsum('tlkb,tlc->lkbc', act_stack, grads, preferred_element_type=jnp...  95.5 us
    squeeze x10, local copies, waits for them, and re-layouts, transpose_apply(): summed = summed + local_flip(terms[:, :, k], s, 1)  81 us
  transfers between devices with their start and end apart: 41, of which 26 were waited for; matrix products, arithmetic and copies ran while one was open for 22% of the time, Pallas kernels for 0%

commit v1 on v0

v1 whole, which is shorter than its diff:
```python
import functools

import jax
import jax.numpy as jnp
from jax import lax
from jax.experimental import pallas as pl
from jax.experimental.pallas import tpu as pltpu
from jax.sharding import PartitionSpec as P

ROOT_HALF = 0.7071067811865476
INV_ROOT_TWO_PI = 0.3989422804014327
VMEM_LIMIT = 48 * 1024 * 1024


def offsets_table(count):
    return [0] + [2**j for j in range(count - 1)]


def split_offsets(count, width):
    table = list(enumerate(offsets_table(count)))
    local = [(k, s) for k, s in table if s < width]
    remote = [(k, s // width) for k, s in table if s >= width]
    return local, remote


def swapped(block, distance):
    count = lax.axis_size("tensor")
    return lax.ppermute(block, "tensor", [(i, i ^ distance) for i in range(count)])


def passed_along(x, by):
    size = lax.axis_size("pipe")
    return lax.ppermute(x, "pipe", [(i, i + by) for i in range(size) if 0 <= i + by < size])


def gelu_value(v):
    return v * 0.5 * (1.0 + lax.erf(v * ROOT_HALF))


def gelu_slope(v):
    return 0.5 * (1.0 + lax.erf(v * ROOT_HALF)) + v * INV_ROOT_TWO_PI * jnp.exp(-0.5 * v * v)


def apply_body(local, transpose, v_ref, *refs):
    w_refs, out_ref = refs[:-1], refs[-1]
    i = pl.program_id(0)
    dims = (((1,), (1 if transpose else 0,)), ((), ()))
    total = None
    for (_, s), w_ref in zip(local, w_refs):
        term = lax.dot_general(v_ref[i ^ s], w_ref[0, 0], dims, preferred_element_type=jnp.float32)
        total = term if total is None else total + term
    out_ref[0] = total


def weight_map(k, s, i):
    return (i ^ s, k, 0, 0)


def local_apply(v, w, local, transpose):
    blocks, tok, bs = v.shape
    return pl.pallas_call(
        functools.partial(apply_body, local, transpose),
        out_shape=jax.ShapeDtypeStruct(v.shape, jnp.float32),
        grid=(blocks,),
        in_specs=[pl.BlockSpec((blocks, tok, bs), lambda i: (0, 0, 0))]
        + [
            pl.BlockSpec((1, 1, bs, bs), functools.partial(weight_map, k, s if transpose else 0))
            for k, s in local
        ],
        out_specs=pl.BlockSpec((1, tok, bs), lambda i: (i, 0, 0)),
        compiler_params=pltpu.CompilerParams(vmem_limit_bytes=VMEM_LIMIT),
        cost_estimate=pl.CostEstimate(
            flops=2 * blocks * len(local) * tok * bs * bs,
            bytes_accessed=blocks * (len(local) * bs * bs * 2 + tok * bs * 6),
            transcendentals=0,
        ),
    )(v, *[w for _ in local])


def grad_body(local, remote, v_ref, g_ref, *refs):
    out_ref = refs[-1]
    i = pl.program_id(0)
    bs = g_ref.shape[-1]
    g = g_ref[...].reshape(-1, bs)
    dims = (((0,), (0,)), ((), ()))
    for k, s in local:
        v = v_ref[:, :, pl.ds(i ^ s, 1)].reshape(-1, bs)
        out_ref[0, k] = lax.dot_general(v, g, dims, preferred_element_type=jnp.float32)
    if remote:
        for pos, (k, _) in enumerate(remote):
            out_ref[0, k] = refs[0][pos, 0].astype(jnp.float32)


def weight_grad(v, g, summed, local, remote):
    dp, micro, blocks, tok, bs = v.shape
    count = len(local) + len(remote)
    in_specs = [
        pl.BlockSpec(v.shape, lambda i: (0, 0, 0, 0, 0)),
        pl.BlockSpec((dp, micro, 1, tok, bs), lambda i: (0, 0, i, 0, 0)),
    ]
    operands = [v, g]
    if remote:
        in_specs.append(pl.BlockSpec((len(remote), 1, bs, bs), lambda i: (0, i, 0, 0)))
        operands.append(summed)
    return pl.pallas_call(
        functools.partial(grad_body, local, remote),
        out_shape=jax.ShapeDtypeStruct((blocks, count, bs, bs), jnp.float32),
        grid=(blocks,),
        in_specs=in_specs,
        out_specs=pl.BlockSpec((1, count, bs, bs), lambda i: (i, 0, 0, 0)),
        compiler_params=pltpu.CompilerParams(vmem_limit_bytes=VMEM_LIMIT),
        cost_estimate=pl.CostEstimate(
            flops=2 * blocks * len(local) * dp * micro * tok * bs * bs,
            bytes_accessed=blocks * (count * bs * bs * 4 + dp * micro * tok * bs * 4),
            transcendentals=0,
        ),
    )(*operands)


def per_device(inputs, cotangent, up_weight, down_weight):
    w_up = up_weight[0]
    w_down = down_weight[0]
    blocks, count, bs = w_up.shape[0], w_up.shape[1], w_up.shape[2]
    micro, tok = inputs.shape[0], inputs.shape[1]
    segment = lax.axis_index("pipe")
    sections = lax.axis_size("pipe")
    steps = micro + sections - 1
    local, remote = split_offsets(count, blocks)

    def to_blocks(x):
        return x.reshape(micro, tok, blocks, bs).transpose(0, 2, 1, 3)

    inputs = to_blocks(inputs)
    cotangent = to_blocks(cotangent)

    def apply_forward(v, w):
        partners = [swapped(v, d) for _, d in remote]
        total = local_apply(v, w, local, False)
        for (k, _), partner in zip(remote, partners):
            total = total + jnp.einsum(
                "ltb,lbc->ltc", partner, w[:, k], preferred_element_type=jnp.float32
            )
        return total, partners

    def apply_transposed(g, w):
        sent = []
        for k, d in remote:
            term = jnp.einsum("ltc,lbc->ltb", g, w[:, k], preferred_element_type=jnp.float32)
            sent.append(swapped(term.astype(jnp.bfloat16), d))
        total = local_apply(g, w, local, True)
        for term in sent:
            total = total + term.astype(jnp.float32)
        return total

    kept = []
    outgoing = None
    for step in range(steps):
        own = inputs[min(step, micro - 1)]
        if step == 0:
            layer_in = own
        else:
            layer_in = jnp.where(segment == 0, own, passed_along(outgoing, 1))
        hidden, in_partners = apply_forward(layer_in, w_up)
        act = gelu_value(hidden).astype(jnp.bfloat16)
        mixed, act_partners = apply_forward(act, w_down)
        outgoing = (layer_in.astype(jnp.float32) + mixed).astype(jnp.bfloat16)
        kept.append((layer_in, act, hidden, in_partners, act_partners))

    kept = jax.tree.map(lambda *xs: jnp.stack(xs), *kept)
    own_kept = jax.tree.map(lambda x: lax.dynamic_slice_in_dim(x, segment, micro, 0), kept)
    z, act, hidden, z_partners, act_partners = own_kept
    z_all = lax.all_gather(z, "dp")
    act_all = lax.all_gather(act, "dp")

    made = []
    for step in range(steps):
        index = jnp.clip(step - (sections - 1 - segment), 0, micro - 1)
        own = cotangent[min(step, micro - 1)]
        if step == 0:
            grads = own
        else:
            grads = jnp.where(segment == sections - 1, own, passed_along(outgoing, -1))
        grad_act = apply_transposed(grads, w_down)
        slope = gelu_slope(lax.dynamic_index_in_dim(hidden, index, 0, keepdims=False))
        grad_hidden = (grad_act * slope).astype(jnp.bfloat16)
        made.append((grads, grad_hidden))
        if step < steps - 1:
            outgoing = (
                grads.astype(jnp.float32) + apply_transposed(grad_hidden, w_up)
            ).astype(jnp.bfloat16)

    made = jax.tree.map(lambda *xs: jnp.stack(xs), *made)
    g, grad_hidden = jax.tree.map(
        lambda x: lax.dynamic_slice_in_dim(x, sections - 1 - segment, micro, 0), made
    )
    g_all = lax.all_gather(g, "dp")
    grad_hidden_all = lax.all_gather(grad_hidden, "dp")

    up_sum = down_sum = None
    if remote:

        def remote_sum(partners, grads):
            return jnp.stack(
                [
                    jnp.einsum("mltb,mltc->lbc", p, grads, preferred_element_type=jnp.float32)
                    for p in partners
                ]
            ).astype(jnp.bfloat16)

        down_sum = lax.psum(remote_sum(act_partners, g), "dp")
        up_sum = lax.psum(remote_sum(z_partners, grad_hidden), "dp")
    grad_down = weight_grad(act_all, g_all, down_sum, local, remote)
    grad_up = weight_grad(z_all, grad_hidden_all, up_sum, local, remote)
    return grad_up[None], grad_down[None]


def solution(mesh):
    in_specs = (
        P(None, "dp", "tensor"),
        P(None, "dp", "tensor"),
        P("pipe", "tensor", None, None, None),
        P("pipe", "tensor", None, None, None),
    )
    out_specs = (P("pipe", "tensor", None, None, None), P("pipe", "tensor", None, None, None))
    return jax.shard_map(
        per_device, mesh=mesh, in_specs=in_specs, out_specs=out_specs, check_vma=False
    )
```

time: 3240 us -> 1250 us (0.39)
  waiting for transfers between devices: 1990 us -> 747 us
  local copies, waits for them, and re-layouts: 672 us -> 46.9 us
  matrix products: 406 us -> 66.7 us
  Pallas kernels: 0 us -> 269 us
  other arithmetic: 81.5 us -> 43.9 us
    psum x1, waiting for transfers between devices: 1650 us -> 159 us  [per_device(): up_sum = lax.psum(remote_sum(z_partners, grad_hidden), 'dp')]
    all_gather x0 -> x4, waiting for transfers between devices: none -> 424 us  [the longest x1 151 us: per_device(): g_all = lax.all_gather(g, 'dp')]
    dot_general x30 -> x20, matrix products: 406 us -> 66.7 us  [the longest x9 31.1 us: apply_forward(): jnp.einsum('ltb,lbc->ltc', partner, w[:, k], preferred_element_type=jnp.f...]
    pallas_call x0 -> x20, Pallas kernels: none -> 269 us  [the longest x18 222 us: local_apply(): pl.pallas_call(functools.partial(apply_body, local, transpose), out_shape...]
    gather x120 -> x0, local copies, waits for them, and re-layouts: 255 us -> none  [local_flip(): jnp.take(values, np.array([j ^ shift_by for j in range(width)], dtype=np....]
    ppermute x40 -> x27, waiting for transfers between devices: 335 us -> 162 us  [the longest x8 92 us: passed_along(): lax.ppermute(x, 'pipe', [(i, i + by) for i in range(size) if 0 <= i + by...]
    while x250 -> x0, local copies, waits for them, and re-layouts: 142 us -> none
    squeeze x15 -> x1, local copies, waits for them, and re-layouts: 87.4 us -> 1.52 us  [per_device(): own = inputs[min(step, micro - 1)]]
  transfers between devices with their start and end apart: 41 -> 32, of which waited for: 26 -> 27; matrix products, arithmetic and copies ran while one was open for 22% -> 7% of each run, Pallas kernels for 0% -> 20%
where the time goes in v1:
time: 1250 us; the launch traced here: 1240 us
  waiting for transfers between devices  747 us (60%)
  Pallas kernels  269 us (22%)
  matrix products  66.7 us (5%)
  starting transfers between devices  50 us (4%)
  local copies, waits for them, and re-layouts  46.9 us (4%)
  other arithmetic  43.9 us (4%)
  between operations  14.5 us (1%)
    pallas_call x18, Pallas kernels, local_apply(): pl.pallas_call(functools.partial(apply_body, local, transpose), out_shape...  222 us
    psum x1, waiting for transfers between devices, per_device(): up_sum = lax.psum(remote_sum(z_partners, grad_hidden), 'dp')  159 us
    all_gather x1, waiting for transfers between devices, per_device(): g_all = lax.all_gather(g, 'dp')  151 us
    all_gather x1, waiting for transfers between devices, per_device(): grad_hidden_all = lax.all_gather(grad_hidden, 'dp')  149 us
    all_gather x1, waiting for transfers between devices, per_device(): z_all = lax.all_gather(z, 'dp')  124 us
    ppermute x8, waiting for transfers between devices, passed_along(): lax.ppermute(x, 'pipe', [(i, i + by) for i in range(size) if 0 <= i + by...  92 us
    ppermute x19, waiting for transfers between devices, swapped(): lax.ppermute(block, 'tensor', [(i, i ^ distance) for i in range(count)])  70.4 us
    pallas_call x2, Pallas kernels, weight_grad(): pl.pallas_call(functools.partial(grad_body, local, remote), out_shape=jax...  47.2 us
  transfers between devices with their start and end apart: 32, of which 27 were waited for; matrix products, arithmetic and copies ran while one was open for 7% of the time, Pallas kernels for 20%

profile of v1, /device:TPU:1, one launch (start us, length us, event | category | flops | bytes accessed | tf_op | source)
XLA Modules:
  0.0 1238.1 jit_solution(9574524333703338976)
XLA Ops:
  77.3 12.0 collective-permute-done.2
  138.3 11.7 collective-permute-done.5
  198.4 11.7 collective-permute-done.8
  243.7 12.2 shard_map.66
  272.1 12.9 %shard_map.67 = f32[16,128,256]{2,1,0:T(8,128)S(1)} custom-call(bf16[16,128,256]{2,1,0:T(8,128)(2,1)S(1)} %get-tuple-element.39.v_ref, bf16[16,6,256,256]{3,2,1,0:T(8,128)(2,1)} %bitcast.334, bf16[16,6,256,256]{3,2,1,0:T(8,128)(2,1)} %bitcast.333, bf16[16,6,256,256]{3,2,1,0:T(8,128)(2,1)} %bitcast.335, bf16[16,6,256,256]{3,2,1,0:T(8,128)(2,1)} %bitcast.336, ...), custom_call_target="tpu_custom_call" | custom-call | flops 1342177280 | bytes 13631488 | tf_op jit(solution)/shard_map/pallas_call | solution.py:61
  297.7 11.7 shard_map.68
  323.9 13.0 %shard_map.69 = f32[16,128,256]{2,1,0:T(8,128)S(1)} custom-call(bf16[16,128,256]{2,1,0:T(8,128)(2,1)S(1)} %get-tuple-element.29.v_ref, bf16[16,6,256,256]{3,2,1,0:T(8,128)(2,1)} %bitcast.285, bf16[16,6,256,256]{3,2,1,0:T(8,128)(2,1)} %bitcast.286, bf16[16,6,256,256]{3,2,1,0:T(8,128)(2,1)} %bitcast.287, bf16[16,6,256,256]{3,2,1,0:T(8,128)(2,1)} %bitcast.288, ...), custom_call_target="tpu_custom_call" | custom-call | flops 1342177280 | bytes 13631488 | tf_op jit(solution)/shard_map/pallas_call | solution.py:61
  350.2 14.8 %collective-permute-done.15 = bf16[16,128,256]{2,1,0:T(8,128)(2,1)S(1)} collective-permute-done((bf16[16,128,256]{2,1,0:T(8,128)(2,1)}, bf16[16,128,256]{2,1,0:T(8,128)(2,1)S(1)}, u32[]{:S(2)}, u32[]{:S(2)}) %collective-permute-start.15) | collective-permute-done | bytes 1048608 | tf_op jit(solution)/shard_map/ppermute | solution.py:33
  373.4 12.8 %shard_map.70 = f32[16,128,256]{2,1,0:T(8,128)S(1)} custom-call(bf16[16,128,256]{2,1,0:T(8,128)(2,1)S(1)} %get-tuple-element.21.v_ref, bf16[16,6,256,256]{3,2,1,0:T(8,128)(2,1)} %bitcast.339, bf16[16,6,256,256]{3,2,1,0:T(8,128)(2,1)} %bitcast.340, bf16[16,6,256,256]{3,2,1,0:T(8,128)(2,1)} %bitcast.341, bf16[16,6,256,256]{3,2,1,0:T(8,128)(2,1)} %bitcast.342, ...), custom_call_target="tpu_custom_call" | custom-call | flops 1342177280 | bytes 13631488 | tf_op jit(solution)/shard_map/pallas_call | solution.py:61
  395.3 12.8 %shard_map.71 = f32[16,128,256]{2,1,0:T(8,128)S(1)} custom-call(bf16[16,128,256]{2,1,0:T(8,128)(2,1)S(1)} %get-tuple-element.27.v_ref, bf16[16,6,256,256]{3,2,1,0:T(8,128)(2,1)} %bitcast.293, bf16[16,6,256,256]{3,2,1,0:T(8,128)(2,1)} %bitcast.292, bf16[16,6,256,256]{3,2,1,0:T(8,128)(2,1)} %bitcast.291, bf16[16,6,256,256]{3,2,1,0:T(8,128)(2,1)} %bitcast.294, ...), custom_call_target="tpu_custom_call" | custom-call | flops 1342177280 | bytes 13631488 | tf_op jit(solution)/shard_map/pallas_call | solution.py:61
  415.3 15.2 %collective-permute-done.18 = bf16[16,128,256]{2,1,0:T(8,128)(2,1)S(1)} collective-permute-done((bf16[16,128,256]{2,1,0:T(8,128)(2,1)}, bf16[16,128,256]{2,1,0:T(8,128)(2,1)S(1)}, u32[]{:S(2)}, u32[]{:S(2)}) %collective-permute-start.18) | collective-permute-done | bytes 1048608 | tf_op jit(solution)/shard_map/ppermute | solution.py:33
  437.9 12.8 %shard_map.72 = f32[16,128,256]{2,1,0:T(8,128)S(1)} custom-call(bf16[16,128,256]{2,1,0:T(8,128)(2,1)S(1)} %get-tuple-element.19.v_ref, bf16[16,6,256,256]{3,2,1,0:T(8,128)(2,1)} %bitcast.348, bf16[16,6,256,256]{3,2,1,0:T(8,128)(2,1)} %bitcast.346, bf16[16,6,256,256]{3,2,1,0:T(8,128)(2,1)} %bitcast.347, bf16[16,6,256,256]{3,2,1,0:T(8,128)(2,1)} %bitcast.345, ...), custom_call_target="tpu_custom_call" | custom-call | flops 1342177280 | bytes 13631488 | tf_op jit(solution)/shard_map/pallas_call | solution.py:61
  463.4 12.8 %shard_map.73 = f32[16,128,256]{2,1,0:T(8,128)S(1)} custom-call(bf16[16,128,256]{2,1,0:T(8,128)(2,1)S(1)} %get-tuple-element.25.v_ref, bf16[16,6,256,256]{3,2,1,0:T(8,128)(2,1)} %bitcast.297, bf16[16,6,256,256]{3,2,1,0:T(8,128)(2,1)} %bitcast.298, bf16[16,6,256,256]{3,2,1,0:T(8,128)(2,1)} %bitcast.299, bf16[16,6,256,256]{3,2,1,0:T(8,128)(2,1)} %bitcast.300, ...), custom_call_target="tpu_custom_call" | custom-call | flops 1342177280 | bytes 13631488 | tf_op jit(solution)/shard_map/pallas_call | solution.py:61
  479.9 14.6 %collective-permute-done.21 = bf16[16,128,256]{2,1,0:T(8,128)(2,1)S(1)} collective-permute-done((bf16[16,128,256]{2,1,0:T(8,128)(2,1)S(1)}, bf16[16,128,256]{2,1,0:T(8,128)(2,1)S(1)}, u32[]{:S(2)}, u32[]{:S(2)}) %collective-permute-start.21) | collective-permute-done | bytes 1048608 | tf_op jit(solution)/shard_map/ppermute | solution.py:33
  499.5 12.8 %shard_map.74 = f32[16,128,256]{2,1,0:T(8,128)S(1)} custom-call(bf16[16,128,256]{2,1,0:T(8,128)(2,1)S(1)} %get-tuple-element.17.v_ref, bf16[16,6,256,256]{3,2,1,0:T(8,128)(2,1)} %bitcast.351, bf16[16,6,256,256]{3,2,1,0:T(8,128)(2,1)} %bitcast.352, bf16[16,6,256,256]{3,2,1,0:T(8,128)(2,1)} %bitcast.353, bf16[16,6,256,256]{3,2,1,0:T(8,128)(2,1)} %bitcast.354, ...), custom_call_target="tpu_custom_call" | custom-call | flops 1342177280 | bytes 13631488 | tf_op jit(solution)/shard_map/pallas_call | solution.py:61
  525.2 12.8 %shard_map.75 = f32[16,128,256]{2,1,0:T(8,128)S(1)} custom-call(bf16[16,128,256]{2,1,0:T(8,128)(2,1)S(1)} %get-tuple-element.23.v_ref, bf16[16,6,256,256]{3,2,1,0:T(8,128)(2,1)} %bitcast.303, bf16[16,6,256,256]{3,2,1,0:T(8,128)(2,1)} %bitcast.304, bf16[16,6,256,256]{3,2,1,0:T(8,128)(2,1)} %bitcast.305, bf16[16,6,256,256]{3,2,1,0:T(8,128)(2,1)} %bitcast.306, ...), custom_call_target="tpu_custom_call" | custom-call | flops 1342177280 | bytes 13631488 | tf_op jit(solution)/shard_map/pallas_call | solution.py:61
  545.2 11.9 collective-permute-done.24
  564.9 13.4 %shard_map.76 = f32[16,128,256]{2,1,0:T(8,128)S(1)} custom-call(bf16[16,128,256]{2,1,0:T(8,128)(2,1)S(1)} %get-tuple-element.15.v_ref, bf16[16,6,256,256]{3,2,1,0:T(8,128)(2,1)} %bitcast.357, bf16[16,6,256,256]{3,2,1,0:T(8,128)(2,1)} %bitcast.358, bf16[16,6,256,256]{3,2,1,0:T(8,128)(2,1)} %bitcast.359, bf16[16,6,256,256]{3,2,1,0:T(8,128)(2,1)} %bitcast.360, ...), custom_call_target="tpu_custom_call" | custom-call | flops 1342177280 | bytes 13631488 | tf_op jit(solution)/shard_map/pallas_call | solution.py:61
  599.5 159.2 %all-reduce.3.cloned.1.call-done = (bf16[1,16,256,256]{3,2,1,0:T(8,128)(2,1)}, bf16[1,16,256,256]{3,2,1,0:T(8,128)(2,1)}) async-done(((bf16[1,16,256,256]{3,2,1,0:T(8,128)(2,1)}, bf16[1,16,256,256]{3,2,1,0:T(8,128)(2,1)}), (bf16[1,16,256,256]{3,2,1,0:T(8,128)(2,1)}, bf16[1,16,256,256]{3,2,1,0:T(8,128)(2,1)})) %all-reduce.3.cloned.1.call-update) | async-done | bytes 4194320 | tf_op jit(solution)/shard_map/psum | solution.py:211
  758.8 150.6 %all-gather.15.cloned.1.call-done = bf16[8,16,128,256]{3,2,1,0:T(8,128)(2,1)} async-done(((bf16[2,16,128,256]{3,2,1,0:T(8,128)(2,1)}), bf16[8,16,128,256]{3,2,1,0:T(8,128)(2,1)}) %all-gather.15.cloned.1.call-update) | async-done | bytes 8388624 | tf_op jit(solution)/shard_map/all_gather | solution.py:196
  910.9 23.7 %shard_map.78 = f32[16,6,256,256]{3,2,1,0:T(8,128)} custom-call(bf16[4,2,16,128,256]{4,3,2,1,0:T(8,128)(2,1)} %bitcast.379, bf16[4,2,16,128,256]{4,3,2,1,0:T(8,128)(2,1)} %bitcast.380, bf16[1,16,256,256]{3,2,1,0:T(8,128)(2,1)S(1)} %copy-done.5), custom_call_target="tpu_custom_call" | custom-call | flops 10737418240 | bytes 41943040 | tf_op jit(solution)/shard_map/pallas_call | solution.py:105
  934.6 124.1 %all-gather.9.cloned.1.call-done = bf16[8,16,128,256]{3,2,1,0:T(8,128)(2,1)} async-done(((bf16[2,16,128,256]{3,2,1,0:T(8,128)(2,1)}), bf16[8,16,128,256]{3,2,1,0:T(8,128)(2,1)}) %all-gather.9.cloned.1.call-update) | async-done | bytes 8388624 | tf_op jit(solution)/shard_map/all_gather | solution.py:172
  1058.7 149.4 %all-gather.11.cloned.1.call-done = bf16[8,16,128,256]{3,2,1,0:T(8,128)(2,1)} async-done(((bf16[2,16,128,256]{3,2,1,0:T(8,128)(2,1)}), bf16[8,16,128,256]{3,2,1,0:T(8,128)(2,1)}) %all-gather.11.cloned.1.call-update) | async-done | bytes 8388624 | tf_op jit(solution)/shard_map/all_gather | solution.py:197
  1208.1 23.4 %shard_map.77 = f32[16,6,256,256]{3,2,1,0:T(8,128)} custom-call(bf16[4,2,16,128,256]{4,3,2,1,0:T(8,128)(2,1)} %bitcast.381, bf16[4,2,16,128,256]{4,3,2,1,0:T(8,128)(2,1)} %bitcast.382, bf16[1,16,256,256]{3,2,1,0:T(8,128)(2,1)S(1)} %copy-done.4), custom_call_target="tpu_custom_call" | custom-call | flops 10737418240 | bytes 41943040 | tf_op jit(solution)/shard_map/pallas_call | solution.py:105
  (214 shorter events, 361.2 us)
Async XLA Ops:
  7.2 592.4 %all-gather.13.cloned.1.call-start = ((), (), s32[]{:S(2)}) async-start(), calls=%async_computation.2 | async-start | bytes 10485760 | tf_op jit(solution)/shard_map/all_gather | solution.py:173
  15.7 25.0 %collective-permute-start = (bf16[16,128,256]{2,1,0:T(8,128)(2,1)S(1)}, bf16[16,128,256]{2,1,0:T(8,128)(2,1)S(1)}, u32[]{:S(2)}, u32[]{:S(2)}) collective-permute-start(bf16[16,128,256]{2,1,0:T(8,128)(2,1)S(1)} %get-tuple-element.40.v_ref), channel_id=1, source_target_pairs={{0,1},{1,0},{2,3},{3,2},{4,5},{5,4},{6,7},{7,6},{8,9},{9,8},{10,11... | collective-permute-start | bytes 3145736 | tf_op jit(solution)/shard_map/ppermute | solution.py:28
  45.0 23.4 %collective-permute-start.1 = (bf16[16,128,256]{2,1,0:T(8,128)(2,1)S(1)}, bf16[16,128,256]{2,1,0:T(8,128)(2,1)S(1)}, u32[]{:S(2)}, u32[]{:S(2)}) collective-permute-start(bf16[16,128,256]{2,1,0:T(8,128)(2,1)S(1)} %get-tuple-element.13.v_ref), channel_id=1, source_target_pairs={{0,1},{1,0},{2,3},{3,2},{4,5},{5,4},{6,7},{7,6},{8,9},{9,8},{10,11... | collective-permute-start | bytes 3145736 | tf_op jit(solution)/shard_map/ppermute | solution.py:28
  72.3 17.1 %collective-permute-start.2 = (bf16[16,128,256]{2,1,0:T(8,128)(2,1)}, bf16[16,128,256]{2,1,0:T(8,128)(2,1)S(1)}, u32[]{:S(2)}, u32[]{:S(2)}) collective-permute-start(bf16[16,128,256]{2,1,0:T(8,128)(2,1)} %add_convert_fusion.7), channel_id=1, source_target_pairs={{0,2},{2,4},{4,6},{1,3},{3,5},{5,7},{8,10},{10,12},{12,14},{9,11},... | collective-permute-start | bytes 3145736 | tf_op jit(solution)/shard_map/ppermute | solution.py:33
  90.7 17.4 %collective-permute-start.3 = (bf16[16,128,256]{2,1,0:T(8,128)(2,1)S(1)}, bf16[16,128,256]{2,1,0:T(8,128)(2,1)S(1)}, u32[]{:S(2)}, u32[]{:S(2)}) collective-permute-start(bf16[16,128,256]{2,1,0:T(8,128)(2,1)S(1)} %get-tuple-element.37.v_ref), channel_id=1, source_target_pairs={{0,1},{1,0},{2,3},{3,2},{4,5},{5,4},{6,7},{7,6},{8,9},{9,8},{10,11... | collective-permute-start | bytes 3145736 | tf_op jit(solution)/shard_map/ppermute | solution.py:28
  130.9 19.1 %collective-permute-start.5 = (bf16[16,128,256]{2,1,0:T(8,128)(2,1)S(1)}, bf16[16,128,256]{2,1,0:T(8,128)(2,1)S(1)}, u32[]{:S(2)}, u32[]{:S(2)}) collective-permute-start(bf16[16,128,256]{2,1,0:T(8,128)(2,1)S(1)} %add_convert_fusion.6), channel_id=1, source_target_pairs={{0,2},{2,4},{4,6},{1,3},{3,5},{5,7},{8,10},{10,12},{12,14},{9,11},... | collective-permute-start | bytes 3145736 | tf_op jit(solution)/shard_map/ppermute | solution.py:33
  151.4 19.9 %collective-permute-start.6 = (bf16[16,128,256]{2,1,0:T(8,128)(2,1)S(1)}, bf16[16,128,256]{2,1,0:T(8,128)(2,1)S(1)}, u32[]{:S(2)}, u32[]{:S(2)}) collective-permute-start(bf16[16,128,256]{2,1,0:T(8,128)(2,1)S(1)} %get-tuple-element.35.v_ref), channel_id=1, source_target_pairs={{0,1},{1,0},{2,3},{3,2},{4,5},{5,4},{6,7},{7,6},{8,9},{9,8},{10,11... | collective-permute-start | bytes 3145736 | tf_op jit(solution)/shard_map/ppermute | solution.py:28
  192.2 17.9 %collective-permute-start.8 = (bf16[16,128,256]{2,1,0:T(8,128)(2,1)S(1)}, bf16[16,128,256]{2,1,0:T(8,128)(2,1)S(1)}, u32[]{:S(2)}, u32[]{:S(2)}) collective-permute-start(bf16[16,128,256]{2,1,0:T(8,128)(2,1)S(1)} %add_convert_fusion.5), channel_id=1, source_target_pairs={{0,2},{2,4},{4,6},{1,3},{3,5},{5,7},{8,10},{10,12},{12,14},{9,11},... | collective-permute-start | bytes 3145736 | tf_op jit(solution)/shard_map/ppermute | solution.py:33
  211.5 18.4 %collective-permute-start.9 = (bf16[16,128,256]{2,1,0:T(8,128)(2,1)S(1)}, bf16[16,128,256]{2,1,0:T(8,128)(2,1)S(1)}, u32[]{:S(2)}, u32[]{:S(2)}) collective-permute-start(bf16[16,128,256]{2,1,0:T(8,128)(2,1)S(1)} %get-tuple-element.33.v_ref), channel_id=1, source_target_pairs={{0,1},{1,0},{2,3},{3,2},{4,5},{5,4},{6,7},{7,6},{8,9},{9,8},{10,11... | collective-permute-start | bytes 3145736 | tf_op jit(solution)/shard_map/ppermute | solution.py:28
  234.4 21.4 %collective-permute-start.10 = (bf16[16,128,256]{2,1,0:T(8,128)(2,1)}, bf16[16,128,256]{2,1,0:T(8,128)(2,1)}, u32[]{:S(2)}, u32[]{:S(2)}) collective-permute-start(bf16[16,128,256]{2,1,0:T(8,128)(2,1)} %get-tuple-element.7.v_ref), channel_id=1, source_target_pairs={{0,1},{1,0},{2,3},{3,2},{4,5},{5,4},{6,7},{7,6},{8,9},{9,8},{10,11... | collective-permute-start | bytes 3145736 | tf_op jit(solution)/shard_map/ppermute | solution.py:28
  259.7 26.9 %collective-permute-start.11 = (bf16[16,128,256]{2,1,0:T(8,128)(2,1)}, bf16[16,128,256]{2,1,0:T(8,128)(2,1)S(1)}, u32[]{:S(2)}, u32[]{:S(2)}) collective-permute-start(bf16[16,128,256]{2,1,0:T(8,128)(2,1)} %add_convert_fusion.4), channel_id=1, source_target_pairs={{0,2},{2,4},{4,6},{1,3},{3,5},{5,7},{8,10},{10,12},{12,14},{9,11},... | collective-permute-start | bytes 3145736 | tf_op jit(solution)/shard_map/ppermute | solution.py:33
  269.5 48.6 %collective-permute-start.12 = (bf16[16,128,256]{2,1,0:T(8,128)(2,1)}, bf16[16,128,256]{2,1,0:T(8,128)(2,1)}, u32[]{:S(2)}, u32[]{:S(2)}) collective-permute-start(bf16[16,128,256]{2,1,0:T(8,128)(2,1)} %convolution_convert_fusion.8), channel_id=1, source_target_pairs={{0,1},{1,0},{2,3},{3,2},{4,5},{5,4},{6,7},{7,6},{8,9},{9,8},{10,11... | collective-permute-start | bytes 3145736 | tf_op jit(solution)/shard_map/ppermute | solution.py:28
  288.7 24.8 %collective-permute-start.13 = (bf16[16,128,256]{2,1,0:T(8,128)(2,1)S(1)}, bf16[16,128,256]{2,1,0:T(8,128)(2,1)S(1)}, u32[]{:S(2)}, u32[]{:S(2)}) collective-permute-start(bf16[16,128,256]{2,1,0:T(8,128)(2,1)S(1)} %get-tuple-element.31.v_ref), channel_id=1, source_target_pairs={{0,1},{1,0},{2,3},{3,2},{4,5},{5,4},{6,7},{7,6},{8,9},{9,8},{10,11... | collective-permute-start | bytes 3145736 | tf_op jit(solution)/shard_map/ppermute | solution.py:28
  323.6 23.2 %collective-permute-start.14 = (bf16[16,128,256]{2,1,0:T(8,128)(2,1)S(1)}, bf16[16,128,256]{2,1,0:T(8,128)(2,1)S(1)}, u32[]{:S(2)}, u32[]{:S(2)}) collective-permute-start(bf16[16,128,256]{2,1,0:T(8,128)(2,1)S(1)} %convolution_convert_fusion.7), channel_id=1, source_target_pairs={{0,1},{1,0},{2,3},{3,2},{4,5},{5,4},{6,7},{7,6},{8,9},{9,8},{10,11... | collective-permute-start | bytes 3145736 | tf_op jit(solution)/shard_map/ppermute | solution.py:28
  410.0 20.4 %collective-permute-start.18 = (bf16[16,128,256]{2,1,0:T(8,128)(2,1)}, bf16[16,128,256]{2,1,0:T(8,128)(2,1)S(1)}, u32[]{:S(2)}, u32[]{:S(2)}) collective-permute-start(bf16[16,128,256]{2,1,0:T(8,128)(2,1)} %add_convert_fusion.2), channel_id=1, source_target_pairs={{2,0},{4,2},{6,4},{3,1},{5,3},{7,5},{10,8},{12,10},{14,12},{11,9},... | collective-permute-start | bytes 3145736 | tf_op jit(solution)/shard_map/ppermute | solution.py:33
  415.0 343.7 %all-reduce.3.cloned.1.call-start = ((), (), s32[]{:S(2)}) async-start(), calls=%async_computation.4 | async-start | bytes 8388608 | tf_op jit(solution)/shard_map/psum | solution.py:211
  437.6 20.2 %collective-permute-start.19 = (bf16[16,128,256]{2,1,0:T(8,128)(2,1)}, bf16[16,128,256]{2,1,0:T(8,128)(2,1)}, u32[]{:S(2)}, u32[]{:S(2)}) collective-permute-start(bf16[16,128,256]{2,1,0:T(8,128)(2,1)} %convolution_convert_fusion.4), channel_id=1, source_target_pairs={{0,1},{1,0},{2,3},{3,2},{4,5},{5,4},{6,7},{7,6},{8,9},{9,8},{10,11... | collective-permute-start | bytes 3145736 | tf_op jit(solution)/shard_map/ppermute | solution.py:28
  521.2 17.3 %collective-permute-start.23 = (bf16[16,128,256]{2,1,0:T(8,128)(2,1)S(1)}, bf16[16,128,256]{2,1,0:T(8,128)(2,1)S(1)}, u32[]{:S(2)}, u32[]{:S(2)}) collective-permute-start(bf16[16,128,256]{2,1,0:T(8,128)(2,1)S(1)} %convolution_convert_fusion.1), channel_id=1, source_target_pairs={{0,1},{1,0},{2,3},{3,2},{4,5},{5,4},{6,7},{7,6},{8,9},{9,8},{10,11... | collective-permute-start | bytes 3145736 | tf_op jit(solution)/shard_map/ppermute | solution.py:28
  539.0 18.2 %collective-permute-start.24 = (bf16[16,128,256]{2,1,0:T(8,128)(2,1)S(1)}, bf16[16,128,256]{2,1,0:T(8,128)(2,1)S(1)}, u32[]{:S(2)}, u32[]{:S(2)}) collective-permute-start(bf16[16,128,256]{2,1,0:T(8,128)(2,1)S(1)} %add_convert_fusion), channel_id=1, source_target_pairs={{2,0},{4,2},{6,4},{3,1},{5,3},{7,5},{10,8},{12,10},{14,12},{11,9},... | collective-permute-start | bytes 3145736 | tf_op jit(solution)/shard_map/ppermute | solution.py:33
  543.6 21.2 %collective-permute-start.26 = (bf16[16,128,256]{2,1,0:T(8,128)(2,1)S(1)}, bf16[16,128,256]{2,1,0:T(8,128)(2,1)S(1)}, u32[]{:S(2)}, u32[]{:S(2)}) collective-permute-start(bf16[16,128,256]{2,1,0:T(8,128)(2,1)S(1)} %copy-done.38), channel_id=1, source_target_pairs={{0,1},{1,0},{2,3},{3,2},{4,5},{5,4},{6,7},{7,6},{8,9},{9,8},{10,11... | collective-permute-start | bytes 3145736 | tf_op jit(solution)/shard_map/ppermute | solution.py:28
  562.0 23.7 %collective-permute-start.25 = (bf16[16,128,256]{2,1,0:T(8,128)(2,1)}, bf16[16,128,256]{2,1,0:T(8,128)(2,1)S(1)}, u32[]{:S(2)}, u32[]{:S(2)}) collective-permute-start(bf16[16,128,256]{2,1,0:T(8,128)(2,1)} %convolution_convert_fusion), channel_id=1, source_target_pairs={{0,1},{1,0},{2,3},{3,2},{4,5},{5,4},{6,7},{7,6},{8,9},{9,8},{10,11... | collective-permute-start | bytes 3145736 | tf_op jit(solution)/shard_map/ppermute | solution.py:28
  595.0 314.3 %all-gather.15.cloned.1.call-start = ((), (), s32[]{:S(2)}) async-start(), calls=%async_computation.3 | async-start | bytes 10485760 | tf_op jit(solution)/shard_map/all_gather | solution.py:196
  595.7 463.0 %all-gather.9.cloned.1.call-start = ((), (), s32[]{:S(2)}) async-start(), calls=%async_computation | async-start | bytes 10485760 | tf_op jit(solution)/shard_map/all_gather | solution.py:172
  598.9 609.2 %all-gather.11.cloned.1.call-start = ((), (), s32[]{:S(2)}) async-start(), calls=%async_computation.1 | async-start | bytes 10485760 | tf_op jit(solution)/shard_map/all_gather | solution.py:197
  (49 other events, 732.2 us)
Sparse Core Ops, SparseCore 0:
  415.1 154.0 all-gather.12
  595.1 163.5 all-reduce.2
  760.4 148.8 all-gather.14
  910.8 147.8 all-gather.8
  1060.2 147.8 all-gather.10

commit v2 on v1

v2 whole, which is shorter than its diff:
```python
import functools

import jax
import jax.numpy as jnp
from jax import lax
from jax.experimental import pallas as pl
from jax.experimental.pallas import tpu as pltpu
from jax.sharding import PartitionSpec as P

ROOT_HALF = 0.7071067811865476
INV_ROOT_TWO_PI = 0.3989422804014327
VMEM_LIMIT = 48 * 1024 * 1024


def offsets_table(count):
    return [0] + [2**j for j in range(count - 1)]


def split_offsets(count, width):
    table = list(enumerate(offsets_table(count)))
    local = [(k, s) for k, s in table if s < width]
    remote = [(k, s // width) for k, s in table if s >= width]
    return local, remote


def swapped(block, distance):
    count = lax.axis_size("tensor")
    return lax.ppermute(block, "tensor", [(i, i ^ distance) for i in range(count)])


def passed_along(x, by):
    size = lax.axis_size("pipe")
    return lax.ppermute(x, "pipe", [(i, i + by) for i in range(size) if 0 <= i + by < size])


def gelu_value(v):
    return v * 0.5 * (1.0 + lax.erf(v * ROOT_HALF))


def gelu_slope(v):
    return 0.5 * (1.0 + lax.erf(v * ROOT_HALF)) + v * INV_ROOT_TWO_PI * jnp.exp(-0.5 * v * v)


def apply_body(local, transpose, v_ref, *refs):
    w_refs, out_ref = refs[: len(local)], refs[-1]
    i = pl.program_id(0)
    dims = (((1,), (1 if transpose else 0,)), ((), ()))
    total = None
    for (_, s), w_ref in zip(local, w_refs):
        term = lax.dot_general(v_ref[i ^ s], w_ref[0, 0], dims, preferred_element_type=jnp.float32)
        total = term if total is None else total + term
    out_ref[0] = total


def weight_map(k, s, i):
    return (i ^ s, k, 0, 0)


def local_apply(v, w, local, transpose, after=()):
    blocks, tok, bs = v.shape
    return pl.pallas_call(
        functools.partial(apply_body, local, transpose),
        out_shape=jax.ShapeDtypeStruct(v.shape, jnp.float32),
        grid=(blocks,),
        in_specs=[pl.BlockSpec((blocks, tok, bs), lambda i: (0, 0, 0))]
        + [
            pl.BlockSpec((1, 1, bs, bs), functools.partial(weight_map, k, s if transpose else 0))
            for k, s in local
        ]
        + [pl.BlockSpec(memory_space=pl.ANY) for _ in after],
        out_specs=pl.BlockSpec((1, tok, bs), lambda i: (i, 0, 0)),
        compiler_params=pltpu.CompilerParams(vmem_limit_bytes=VMEM_LIMIT),
        cost_estimate=pl.CostEstimate(
            flops=2 * blocks * len(local) * tok * bs * bs,
            bytes_accessed=blocks * (len(local) * bs * bs * 2 + tok * bs * 6),
            transcendentals=0,
        ),
    )(v, *[w for _ in local], *after)


def grad_body(local, remote, micro, *refs):
    g_refs, v_refs, out_ref = refs[:micro], refs[micro : 2 * micro], refs[-1]
    partner_refs = refs[2 * micro : -1]
    i = pl.program_id(0)
    bs = out_ref.shape[-1]
    grads = [g[...].reshape(-1, bs) for g in g_refs]
    dims = (((0,), (0,)), ((), ()))

    def product(values):
        total = None
        for v, g in zip(values, grads):
            term = lax.dot_general(v, g, dims, preferred_element_type=jnp.float32)
            total = term if total is None else total + term
        return total

    for k, s in local:
        out_ref[0, k] = product([v[:, pl.ds(i ^ s, 1)].reshape(-1, bs) for v in v_refs])
    for pos, (k, _) in enumerate(remote):
        own = partner_refs[pos * micro : (pos + 1) * micro]
        out_ref[0, k] = product([v[...].reshape(-1, bs) for v in own])


def weight_grad(values, grads, partners, local, remote):
    micro = len(values)
    dp, blocks, tok, bs = values[0].shape
    count = len(local) + len(remote)
    one = pl.BlockSpec((dp, 1, tok, bs), lambda i: (0, i, 0, 0))
    whole = pl.BlockSpec((dp, blocks, tok, bs), lambda i: (0, 0, 0, 0))
    return pl.pallas_call(
        functools.partial(grad_body, local, remote, micro),
        out_shape=jax.ShapeDtypeStruct((blocks, count, bs, bs), jnp.float32),
        grid=(blocks,),
        in_specs=[one] * micro + [whole] * micro + [one] * (micro * len(remote)),
        out_specs=pl.BlockSpec((1, count, bs, bs), lambda i: (i, 0, 0, 0)),
        compiler_params=pltpu.CompilerParams(vmem_limit_bytes=VMEM_LIMIT),
        cost_estimate=pl.CostEstimate(
            flops=2 * blocks * count * dp * micro * tok * bs * bs,
            bytes_accessed=blocks * (count * bs * bs * 4 + dp * micro * tok * bs * 4),
            transcendentals=0,
        ),
    )(*grads, *values, *[p for group in partners for p in group])


def per_device(inputs, cotangent, up_weight, down_weight):
    w_up = up_weight[0]
    w_down = down_weight[0]
    blocks, count, bs = w_up.shape[0], w_up.shape[1], w_up.shape[2]
    micro, tok = inputs.shape[0], inputs.shape[1]
    segment = lax.axis_index("pipe")
    sections = lax.axis_size("pipe")
    steps = micro + sections - 1
    local, remote = split_offsets(count, blocks)

    def to_blocks(x):
        return x.reshape(micro, tok, blocks, bs).transpose(0, 2, 1, 3)

    inputs = to_blocks(inputs)
    cotangent = to_blocks(cotangent)

    def apply_forward(v, w):
        partners = [swapped(v, d) for _, d in remote]
        total = local_apply(v, w, local, False)
        for (k, _), partner in zip(remote, partners):
            total = total + jnp.einsum(
                "ltb,lbc->ltc", partner, w[:, k], preferred_element_type=jnp.float32
            )
        return total

    def apply_transposed(g, w, after=()):
        sent = []
        for k, d in remote:
            term = jnp.einsum("ltc,lbc->ltb", g, w[:, k], preferred_element_type=jnp.float32)
            sent.append(swapped(term.astype(jnp.bfloat16), d))
        total = local_apply(g, w, local, True, after)
        for term in sent:
            total = total + term.astype(jnp.float32)
        return total

    kept = []
    outgoing = None
    for step in range(steps):
        own = inputs[min(step, micro - 1)]
        if step == 0:
            layer_in = own
        else:
            layer_in = jnp.where(segment == 0, own, passed_along(outgoing, 1))
        hidden = apply_forward(layer_in, w_up)
        act = gelu_value(hidden).astype(jnp.bfloat16)
        mixed = apply_forward(act, w_down)
        outgoing = (layer_in.astype(jnp.float32) + mixed).astype(jnp.bfloat16)
        kept.append((layer_in, act, hidden))

    def own_step(items, first, m):
        window = items[m : m + sections]
        return lax.dynamic_index_in_dim(jnp.stack(window), first, 0, keepdims=False)

    def gathered(x):
        return lax.all_gather(x, "dp")

    z_all, act_all = [], []
    for m in range(micro):
        z_all.append(gathered(own_step([x[0] for x in kept], segment, m)))
        act_all.append(gathered(own_step([x[1] for x in kept], segment, m)))
    hidden = jnp.stack([own_step([x[2] for x in kept], segment, m) for m in range(micro)])
    due = [x for pair in zip(z_all, act_all) for x in pair]

    made = []
    for step in range(steps):
        index = jnp.clip(step - (sections - 1 - segment), 0, micro - 1)
        own = cotangent[min(step, micro - 1)]
        if step == 0:
            grads = own
        else:
            grads = jnp.where(segment == sections - 1, own, passed_along(outgoing, -1))
        after = due[step - 1 : step] if step < steps - 1 else due[step - 1 :]
        grad_act = apply_transposed(grads, w_down, after if step else ())
        slope = gelu_slope(lax.dynamic_index_in_dim(hidden, index, 0, keepdims=False))
        grad_hidden = (grad_act * slope).astype(jnp.bfloat16)
        made.append((grads, grad_hidden))
        if step < steps - 1:
            outgoing = (
                grads.astype(jnp.float32) + apply_transposed(grad_hidden, w_up)
            ).astype(jnp.bfloat16)

    g_all, grad_hidden_all = [], []
    last = sections - 1 - segment
    for m in range(micro):
        g_all.append(gathered(own_step([x[0] for x in made], last, m)))
        grad_hidden_all.append(gathered(own_step([x[1] for x in made], last, m)))

    act_partners = [[swapped(x, d) for x in act_all] for _, d in remote]
    z_partners = [[swapped(x, d) for x in z_all] for _, d in remote]
    grad_down = weight_grad(act_all, g_all, act_partners, local, remote)
    grad_up = weight_grad(z_all, grad_hidden_all, z_partners, local, remote)
    return grad_up[None], grad_down[None]


def solution(mesh):
    in_specs = (
        P(None, "dp", "tensor"),
        P(None, "dp", "tensor"),
        P("pipe", "tensor", None, None, None),
        P("pipe", "tensor", None, None, None),
    )
    out_specs = (P("pipe", "tensor", None, None, None), P("pipe", "tensor", None, None, None))
    return jax.shard_map(
        per_device, mesh=mesh, in_specs=in_specs, out_specs=out_specs, check_vma=False
    )
```

time: 1250 us -> 1030 us (0.82)
  waiting for transfers between devices: 747 us -> 545 us
  local copies, waits for them, and re-layouts: 46.9 us -> 22.6 us
  matrix products: 66.7 us -> 49.1 us
    all_gather x4 -> x8, waiting for transfers between devices: 424 us -> 36.7 us  [gathered(): return lax.all_gather(x, 'dp')]
    ppermute x19 -> x22, waiting for transfers between devices: 70.4 us -> 398 us  [swapped(): lax.ppermute(block, 'tensor', [(i, i ^ distance) for i in range(count)])]
    psum x1 -> x0, waiting for transfers between devices: 159 us -> none  [per_device(): up_sum = lax.psum(remote_sum(z_partners, grad_hidden), 'dp')]
    unnamed x14 -> x0, other arithmetic: 29 us -> none
    ppermute x8, waiting for transfers between devices: 92 us -> 109 us  [passed_along(): lax.ppermute(x, 'pipe', [(i, i + by) for i in range(size) if 0 <= i + by...]
    unnamed x94 -> x82, local copies, waits for them, and re-layouts: 27.8 us -> 14.1 us
    convert_element_type x0 -> x7, other arithmetic: none -> 13.2 us  [the longest x4 7.43 us: per_device(): grad_hidden = (grad_act * slope).astype(jnp.bfloat16)]
  transfers between devices with their start and end apart: 32 -> 38, of which waited for: 27 -> 27; matrix products, arithmetic and copies ran while one was open for 7% -> 7% of each run, Pallas kernels for 20% -> 25%
where the time goes in v2:
time: 1030 us; the launch traced here: 1010 us
  waiting for transfers between devices  545 us (53%)
  Pallas kernels  275 us (27%)
  starting transfers between devices  60.1 us (6%)
  matrix products  49.1 us (5%)
  other arithmetic  44.5 us (4%)
  local copies, waits for them, and re-layouts  22.6 us (2%)
  between operations  15.4 us (1%)
    ppermute x22, waiting for transfers between devices, swapped(): lax.ppermute(block, 'tensor', [(i, i ^ distance) for i in range(count)])  398 us
    pallas_call x18, Pallas kernels, local_apply(): pl.pallas_call(functools.partial(apply_body, local, transpose), out_shape...  223 us
    ppermute x8, waiting for transfers between devices, passed_along(): lax.ppermute(x, 'pipe', [(i, i + by) for i in range(size) if 0 <= i + by...  109 us
    pallas_call x2, Pallas kernels, weight_grad(): pl.pallas_call(functools.partial(grad_body, local, remote, micro), out_sh...  52.8 us
    ppermute x8, starting transfers between devices, passed_along(): lax.ppermute(x, 'pipe', [(i, i + by) for i in range(size) if 0 <= i + by...  37.3 us
    all_gather x8, waiting for transfers between devices, gathered(): return lax.all_gather(x, 'dp')  36.7 us
    dot_general x9, matrix products, apply_transposed(): jnp.einsum('ltc,lbc->ltb', g, w[:, k], preferred_element_type=jnp.float32)  29.2 us
    ppermute x22, starting transfers between devices, swapped(): lax.ppermute(block, 'tensor', [(i, i ^ distance) for i in range(count)])  22.3 us
  transfers between devices with their start and end apart: 38, of which 27 were waited for; matrix products, arithmetic and copies ran while one was open for 7% of the time, Pallas kernels for 25%

profile of v2, /device:TPU:1, one launch (start us, length us, event | category | flops | bytes accessed | tf_op | source)
XLA Modules:
  0.0 1012.0 jit_solution(15437717161321680548)
XLA Ops:
  135.2 11.7 %collective-permute-done.6 = bf16[16,128,256]{2,1,0:T(8,128)(2,1)S(1)} collective-permute-done((bf16[16,128,256]{2,1,0:T(8,128)(2,1)S(1)}, bf16[16,128,256]{2,1,0:T(8,128)(2,1)S(1)}, u32[]{:S(2)}, u32[]{:S(2)}) %collective-permute-start.6) | collective-permute-done | bytes 1048608 | tf_op jit(solution)/shard_map/ppermute | solution.py:33
  253.2 11.9 %collective-permute-done.12 = bf16[16,128,256]{2,1,0:T(8,128)(2,1)} collective-permute-done((bf16[16,128,256]{2,1,0:T(8,128)(2,1)}, bf16[16,128,256]{2,1,0:T(8,128)(2,1)}, u32[]{:S(2)}, u32[]{:S(2)}) %collective-permute-start.12) | collective-permute-done | bytes 1048608 | tf_op jit(solution)/shard_map/ppermute | solution.py:33
  282.5 11.7 %shard_map.68 = f32[16,128,256]{2,1,0:T(8,128)S(1)} custom-call(bf16[16,128,256]{2,1,0:T(8,128)(2,1)S(1)} %copy-done.17, bf16[16,6,256,256]{3,2,1,0:T(8,128)(2,1)} %bitcast.170, bf16[16,6,256,256]{3,2,1,0:T(8,128)(2,1)} %bitcast.169, bf16[16,6,256,256]{3,2,1,0:T(8,128)(2,1)} %bitcast.168, bf16[16,6,256,256]{3,2,1,0:T(8,128)(2,1)} %bitcast.171, ...), custom_call_target="tpu_custom_call" | custom-call | flops 1342177280 | bytes 13631488 | tf_op jit(solution)/shard_map/pallas_call | solution.py:61
  303.5 13.0 %shard_map.59 = f32[16,128,256]{2,1,0:T(8,128)S(1)} custom-call(bf16[16,128,256]{2,1,0:T(8,128)(2,1)S(1)} %get-tuple-element.21.v_ref, bf16[16,6,256,256]{3,2,1,0:T(8,128)(2,1)} %bitcast.224, bf16[16,6,256,256]{3,2,1,0:T(8,128)(2,1)} %bitcast.223, bf16[16,6,256,256]{3,2,1,0:T(8,128)(2,1)} %bitcast.225, bf16[16,6,256,256]{3,2,1,0:T(8,128)(2,1)} %bitcast.226, ...), custom_call_target="tpu_custom_call" | custom-call | flops 1342177280 | bytes 13631488 | tf_op jit(solution)/shard_map/pallas_call | solution.py:61
  325.3 12.8 %shard_map.69 = f32[16,128,256]{2,1,0:T(8,128)S(1)} custom-call(bf16[16,128,256]{2,1,0:T(8,128)(2,1)S(1)} %fusion.4.v_ref, bf16[16,6,256,256]{3,2,1,0:T(8,128)(2,1)} %bitcast.175, bf16[16,6,256,256]{3,2,1,0:T(8,128)(2,1)} %bitcast.176, bf16[16,6,256,256]{3,2,1,0:T(8,128)(2,1)} %bitcast.177, bf16[16,6,256,256]{3,2,1,0:T(8,128)(2,1)} %bitcast.178, ...), custom_call_target="tpu_custom_call" | custom-call | flops 1342177280 | bytes 13631488 | tf_op jit(solution)/shard_map/pallas_call | solution.py:61
  340.7 18.9 %collective-permute-done.15 = bf16[16,128,256]{2,1,0:T(8,128)(2,1)} collective-permute-done((bf16[16,128,256]{2,1,0:T(8,128)(2,1)S(1)}, bf16[16,128,256]{2,1,0:T(8,128)(2,1)}, u32[]{:S(2)}, u32[]{:S(2)}) %collective-permute-start.15) | collective-permute-done | bytes 1048608 | tf_op jit(solution)/shard_map/ppermute | solution.py:33
  363.9 13.0 %shard_map.70 = f32[16,128,256]{2,1,0:T(8,128)S(1)} custom-call(bf16[16,128,256]{2,1,0:T(8,128)(2,1)S(1)} %broadcast_select_fusion.3.v_ref, bf16[16,6,256,256]{3,2,1,0:T(8,128)(2,1)} %bitcast.229, bf16[16,6,256,256]{3,2,1,0:T(8,128)(2,1)} %bitcast.230, bf16[16,6,256,256]{3,2,1,0:T(8,128)(2,1)} %bitcast.231, bf16[16,6,256,256]{3,2,1,0:T(8,128)(2,1)} %bitcast.232, ...), custom_call_target="tpu_custom_call" | custom-call | flops 1342177280 | bytes 13631488 | tf_op jit(solution)/shard_map/pallas_call | solution.py:61
  385.4 12.8 %shard_map.71 = f32[16,128,256]{2,1,0:T(8,128)S(1)} custom-call(bf16[16,128,256]{2,1,0:T(8,128)(2,1)S(1)} %fusion.9.v_ref, bf16[16,6,256,256]{3,2,1,0:T(8,128)(2,1)} %bitcast.183, bf16[16,6,256,256]{3,2,1,0:T(8,128)(2,1)} %bitcast.182, bf16[16,6,256,256]{3,2,1,0:T(8,128)(2,1)} %bitcast.181, bf16[16,6,256,256]{3,2,1,0:T(8,128)(2,1)} %bitcast.184, ...), custom_call_target="tpu_custom_call" | custom-call | flops 1342177280 | bytes 13631488 | tf_op jit(solution)/shard_map/pallas_call | solution.py:61
  402.5 14.6 %collective-permute-done.18 = bf16[16,128,256]{2,1,0:T(8,128)(2,1)S(1)} collective-permute-done((bf16[16,128,256]{2,1,0:T(8,128)(2,1)S(1)}, bf16[16,128,256]{2,1,0:T(8,128)(2,1)S(1)}, u32[]{:S(2)}, u32[]{:S(2)}) %collective-permute-start.18) | collective-permute-done | bytes 1048608 | tf_op jit(solution)/shard_map/ppermute | solution.py:33
  421.0 12.5 %all-gather.11.cloned.1.call-done.refs_5_.refs_2_ = bf16[4,16,128,256]{3,2,1,0:T(8,128)(2,1)} async-done(((bf16[1,16,128,256]{3,2,1,0:T(8,128)(2,1)}), bf16[4,16,128,256]{3,2,1,0:T(8,128)(2,1)}) %all-gather.11.cloned.1.call-update) | async-done | bytes 4194320 | tf_op jit(solution)/shard_map/all_gather | solution.py:178
  433.5 13.3 %shard_map.72 = f32[16,128,256]{2,1,0:T(8,128)S(1)} custom-call(bf16[16,128,256]{2,1,0:T(8,128)(2,1)S(1)} %broadcast_select_fusion.2.v_ref, bf16[16,6,256,256]{3,2,1,0:T(8,128)(2,1)} %bitcast.238, bf16[16,6,256,256]{3,2,1,0:T(8,128)(2,1)} %bitcast.236, bf16[16,6,256,256]{3,2,1,0:T(8,128)(2,1)} %bitcast.237, bf16[16,6,256,256]{3,2,1,0:T(8,128)(2,1)} %bitcast.235, ...), custom_call_target="tpu_custom_call" | custom-call | flops 1342177280 | bytes 13631488 | tf_op jit(solution)/shard_map/pallas_call | solution.py:61
  452.1 12.8 %shard_map.73 = f32[16,128,256]{2,1,0:T(8,128)S(1)} custom-call(bf16[16,128,256]{2,1,0:T(8,128)(2,1)S(1)} %fusion.14.v_ref, bf16[16,6,256,256]{3,2,1,0:T(8,128)(2,1)} %bitcast.187, bf16[16,6,256,256]{3,2,1,0:T(8,128)(2,1)} %bitcast.188, bf16[16,6,256,256]{3,2,1,0:T(8,128)(2,1)} %bitcast.189, bf16[16,6,256,256]{3,2,1,0:T(8,128)(2,1)} %bitcast.190, ...), custom_call_target="tpu_custom_call" | custom-call | flops 1342177280 | bytes 13631488 | tf_op jit(solution)/shard_map/pallas_call | solution.py:61
  479.0 13.8 %collective-permute-done.21 = bf16[16,128,256]{2,1,0:T(8,128)(2,1)} collective-permute-done((bf16[16,128,256]{2,1,0:T(8,128)(2,1)S(1)}, bf16[16,128,256]{2,1,0:T(8,128)(2,1)}, u32[]{:S(2)}, u32[]{:S(2)}) %collective-permute-start.21) | collective-permute-done | bytes 1048608 | tf_op jit(solution)/shard_map/ppermute | solution.py:33
  499.0 15.3 %all-gather.13.cloned.1.call-done.refs_5_.refs_3_ = bf16[4,16,128,256]{3,2,1,0:T(8,128)(2,1)} async-done(((bf16[1,16,128,256]{3,2,1,0:T(8,128)(2,1)}), bf16[4,16,128,256]{3,2,1,0:T(8,128)(2,1)}) %all-gather.13.cloned.1.call-update) | async-done | bytes 4194320 | tf_op jit(solution)/shard_map/all_gather | solution.py:178
  514.4 13.3 %shard_map.74 = f32[16,128,256]{2,1,0:T(8,128)S(1)} custom-call(bf16[16,128,256]{2,1,0:T(8,128)(2,1)S(1)} %broadcast_select_fusion.1.v_ref, bf16[16,6,256,256]{3,2,1,0:T(8,128)(2,1)} %bitcast.241, bf16[16,6,256,256]{3,2,1,0:T(8,128)(2,1)} %bitcast.242, bf16[16,6,256,256]{3,2,1,0:T(8,128)(2,1)} %bitcast.243, bf16[16,6,256,256]{3,2,1,0:T(8,128)(2,1)} %bitcast.244, ...), custom_call_target="tpu_custom_call" | custom-call | flops 1342177280 | bytes 13631488 | tf_op jit(solution)/shard_map/pallas_call | solution.py:61
  534.1 12.8 %shard_map.75 = f32[16,128,256]{2,1,0:T(8,128)S(1)} custom-call(bf16[16,128,256]{2,1,0:T(8,128)(2,1)S(1)} %fusion.19.v_ref, bf16[16,6,256,256]{3,2,1,0:T(8,128)(2,1)} %bitcast.193, bf16[16,6,256,256]{3,2,1,0:T(8,128)(2,1)} %bitcast.194, bf16[16,6,256,256]{3,2,1,0:T(8,128)(2,1)} %bitcast.195, bf16[16,6,256,256]{3,2,1,0:T(8,128)(2,1)} %bitcast.196, ...), custom_call_target="tpu_custom_call" | custom-call | flops 1342177280 | bytes 13631488 | tf_op jit(solution)/shard_map/pallas_call | solution.py:61
  561.8 14.2 %collective-permute-done.24 = bf16[16,128,256]{2,1,0:T(8,128)(2,1)} collective-permute-done((bf16[16,128,256]{2,1,0:T(8,128)(2,1)}, bf16[16,128,256]{2,1,0:T(8,128)(2,1)}, u32[]{:S(2)}, u32[]{:S(2)}) %collective-permute-start.24) | collective-permute-done | bytes 1048608 | tf_op jit(solution)/shard_map/ppermute | solution.py:33
  595.1 13.2 %shard_map.76 = f32[16,128,256]{2,1,0:T(8,128)S(1)} custom-call(bf16[16,128,256]{2,1,0:T(8,128)(2,1)S(1)} %copy-done.9, bf16[16,6,256,256]{3,2,1,0:T(8,128)(2,1)} %bitcast.247, bf16[16,6,256,256]{3,2,1,0:T(8,128)(2,1)} %bitcast.248, bf16[16,6,256,256]{3,2,1,0:T(8,128)(2,1)} %bitcast.249, bf16[16,6,256,256]{3,2,1,0:T(8,128)(2,1)} %bitcast.250, ...), custom_call_target="tpu_custom_call" | custom-call | flops 1342177280 | bytes 13631488 | tf_op jit(solution)/shard_map/pallas_call | solution.py:61
  617.6 88.9 %collective-permute-done.28.refs_4_ = bf16[4,16,128,256]{3,2,1,0:T(8,128)(2,1)} collective-permute-done((bf16[4,16,128,256]{3,2,1,0:T(8,128)(2,1)}, bf16[4,16,128,256]{3,2,1,0:T(8,128)(2,1)}, u32[]{:S(2)}, u32[]{:S(2)}) %collective-permute-start.28) | collective-permute-done | bytes 4194336 | tf_op jit(solution)/shard_map/ppermute | solution.py:28
  706.5 89.9 %collective-permute-done.29.refs_5_ = bf16[4,16,128,256]{3,2,1,0:T(8,128)(2,1)} collective-permute-done((bf16[4,16,128,256]{3,2,1,0:T(8,128)(2,1)}, bf16[4,16,128,256]{3,2,1,0:T(8,128)(2,1)}, u32[]{:S(2)}, u32[]{:S(2)}) %collective-permute-start.29) | collective-permute-done | bytes 4194336 | tf_op jit(solution)/shard_map/ppermute | solution.py:28
  798.6 26.5 %shard_map.78 = f32[16,6,256,256]{3,2,1,0:T(8,128)} custom-call(bf16[4,16,128,256]{3,2,1,0:T(8,128)(2,1)S(1)} %copy-done.20, bf16[4,16,128,256]{3,2,1,0:T(8,128)(2,1)} %all-gather.23.cloned.1.call-done.refs_1_, bf16[4,16,128,256]{3,2,1,0:T(8,128)(2,1)} %all-gather.11.cloned.1.call-done.refs_5_.refs_2_, ...), custom_call_target="tpu_custom_call" | custom-call | flops 12884901888 | bytes 41943040 | tf_op jit(solution)/shard_map/pallas_call | solution.py:109
  825.0 61.2 %collective-permute-done.26.refs_4_ = bf16[4,16,128,256]{3,2,1,0:T(8,128)(2,1)} collective-permute-done((bf16[4,16,128,256]{3,2,1,0:T(8,128)(2,1)}, bf16[4,16,128,256]{3,2,1,0:T(8,128)(2,1)}, u32[]{:S(2)}, u32[]{:S(2)}) %collective-permute-start.26) | collective-permute-done | bytes 4194336 | tf_op jit(solution)/shard_map/ppermute | solution.py:28
  886.3 89.9 %collective-permute-done.27.refs_5_ = bf16[4,16,128,256]{3,2,1,0:T(8,128)(2,1)} collective-permute-done((bf16[4,16,128,256]{3,2,1,0:T(8,128)(2,1)}, bf16[4,16,128,256]{3,2,1,0:T(8,128)(2,1)}, u32[]{:S(2)}, u32[]{:S(2)}) %collective-permute-start.27) | collective-permute-done | bytes 4194336 | tf_op jit(solution)/shard_map/ppermute | solution.py:28
  978.4 26.4 %shard_map.77 = f32[16,6,256,256]{3,2,1,0:T(8,128)} custom-call(bf16[4,16,128,256]{3,2,1,0:T(8,128)(2,1)S(1)} %copy-done.21, bf16[4,16,128,256]{3,2,1,0:T(8,128)(2,1)} %all-gather.19.cloned.1.call-done.refs_1_, bf16[4,16,128,256]{3,2,1,0:T(8,128)(2,1)} %all-gather.9.cloned.1.call-done.refs_5_.refs_2_, ...), custom_call_target="tpu_custom_call" | custom-call | flops 12884901888 | bytes 41943040 | tf_op jit(solution)/shard_map/pallas_call | solution.py:109
  (214 shorter events, 372.0 us)
Async XLA Ops:
  7.2 356.8 %all-gather.9.cloned.1.call-start = ((), (), s32[]{:S(2)}) async-start(), calls=%async_computation | async-start | bytes 5242880 | tf_op jit(solution)/shard_map/all_gather | solution.py:178
  15.7 25.0 %collective-permute-start.1 = (bf16[16,128,256]{2,1,0:T(8,128)(2,1)S(1)}, bf16[16,128,256]{2,1,0:T(8,128)(2,1)S(1)}, u32[]{:S(2)}, u32[]{:S(2)}) collective-permute-start(bf16[16,128,256]{2,1,0:T(8,128)(2,1)S(1)} %get-tuple-element.23.v_ref), channel_id=1, source_target_pairs={{0,1},{1,0},{2,3},{3,2},{4,5},{5,4},{6,7},{7,6},{8,9},{9,8},{10,11... | collective-permute-start | bytes 3145736 | tf_op jit(solution)/shard_map/ppermute | solution.py:28
  44.2 23.4 %collective-permute-start.2 = (bf16[16,128,256]{2,1,0:T(8,128)(2,1)S(1)}, bf16[16,128,256]{2,1,0:T(8,128)(2,1)S(1)}, u32[]{:S(2)}, u32[]{:S(2)}) collective-permute-start(bf16[16,128,256]{2,1,0:T(8,128)(2,1)S(1)} %get-tuple-element.24.v_ref), channel_id=1, source_target_pairs={{0,1},{1,0},{2,3},{3,2},{4,5},{5,4},{6,7},{7,6},{8,9},{9,8},{10,11... | collective-permute-start | bytes 3145736 | tf_op jit(solution)/shard_map/ppermute | solution.py:28
  147.0 21.0 %collective-permute-start.7 = (bf16[16,128,256]{2,1,0:T(8,128)(2,1)S(1)}, bf16[16,128,256]{2,1,0:T(8,128)(2,1)S(1)}, u32[]{:S(2)}, u32[]{:S(2)}) collective-permute-start(bf16[16,128,256]{2,1,0:T(8,128)(2,1)S(1)} %broadcast_select_fusion.6.v_ref), channel_id=1, source_target_pairs={{0,1},{1,0},{2,3},{3,2},{4,5},{5,4},{6,7},{7,6},{8,9},{9,8},{10,11... | collective-permute-start | bytes 3145736 | tf_op jit(solution)/shard_map/ppermute | solution.py:28
  245.2 19.9 %collective-permute-start.12 = (bf16[16,128,256]{2,1,0:T(8,128)(2,1)}, bf16[16,128,256]{2,1,0:T(8,128)(2,1)}, u32[]{:S(2)}, u32[]{:S(2)}) collective-permute-start(bf16[16,128,256]{2,1,0:T(8,128)(2,1)} %add_convert_fusion.4), channel_id=1, source_target_pairs={{0,2},{2,4},{4,6},{1,3},{3,5},{5,7},{8,10},{10,12},{12,14},{9,11},... | collective-permute-start | bytes 3145736 | tf_op jit(solution)/shard_map/ppermute | solution.py:33
  269.7 163.8 %all-gather.11.cloned.1.call-start = ((), (), s32[]{:S(2)}) async-start(), calls=%async_computation.1 | async-start | bytes 5242880 | tf_op jit(solution)/shard_map/all_gather | solution.py:178
  269.7 24.6 %collective-permute-start.13 = (bf16[16,128,256]{2,1,0:T(8,128)(2,1)}, bf16[16,128,256]{2,1,0:T(8,128)(2,1)S(1)}, u32[]{:S(2)}, u32[]{:S(2)}) collective-permute-start(bf16[16,128,256]{2,1,0:T(8,128)(2,1)} %copy-done.16), channel_id=1, source_target_pairs={{0,1},{1,0},{2,3},{3,2},{4,5},{5,4},{6,7},{7,6},{8,9},{9,8},{10,11... | collective-permute-start | bytes 3145736 | tf_op jit(solution)/shard_map/ppermute | solution.py:28
  282.3 36.1 %collective-permute-start = (bf16[16,128,256]{2,1,0:T(8,128)(2,1)}, bf16[16,128,256]{2,1,0:T(8,128)(2,1)}, u32[]{:S(2)}, u32[]{:S(2)}) collective-permute-start(bf16[16,128,256]{2,1,0:T(8,128)(2,1)} %convolution_convert_fusion.8), channel_id=1, source_target_pairs={{0,1},{1,0},{2,3},{3,2},{4,5},{5,4},{6,7},{7,6},{8,9},{9,8},{10,11... | collective-permute-start | bytes 3145736 | tf_op jit(solution)/shard_map/ppermute | solution.py:28
  302.2 212.2 %all-gather.13.cloned.1.call-start = ((), (), s32[]{:S(2)}) async-start(), calls=%async_computation.2 | async-start | bytes 5242880 | tf_op jit(solution)/shard_map/all_gather | solution.py:178
  338.6 21.1 %collective-permute-start.15 = (bf16[16,128,256]{2,1,0:T(8,128)(2,1)S(1)}, bf16[16,128,256]{2,1,0:T(8,128)(2,1)}, u32[]{:S(2)}, u32[]{:S(2)}) collective-permute-start(bf16[16,128,256]{2,1,0:T(8,128)(2,1)S(1)} %add_convert_fusion.3), channel_id=1, source_target_pairs={{2,0},{4,2},{6,4},{3,1},{5,3},{7,5},{10,8},{12,10},{14,12},{11,9},... | collective-permute-start | bytes 3145736 | tf_op jit(solution)/shard_map/ppermute | solution.py:33
  385.3 209.8 %all-gather.17.cloned.1.call-start = ((), (), s32[]{:S(2)}) async-start(), calls=%async_computation.4 | async-start | bytes 5242880 | tf_op jit(solution)/shard_map/all_gather | solution.py:178
  420.7 26.1 %collective-permute-start.19 = (bf16[16,128,256]{2,1,0:T(8,128)(2,1)}, bf16[16,128,256]{2,1,0:T(8,128)(2,1)S(1)}, u32[]{:S(2)}, u32[]{:S(2)}) collective-permute-start(bf16[16,128,256]{2,1,0:T(8,128)(2,1)} %convolution_convert_fusion.4), channel_id=1, source_target_pairs={{0,1},{1,0},{2,3},{3,2},{4,5},{5,4},{6,7},{7,6},{8,9},{9,8},{10,11... | collective-permute-start | bytes 3145736 | tf_op jit(solution)/shard_map/ppermute | solution.py:28
  450.9 24.3 %collective-permute-start.20 = (bf16[16,128,256]{2,1,0:T(8,128)(2,1)S(1)}, bf16[16,128,256]{2,1,0:T(8,128)(2,1)S(1)}, u32[]{:S(2)}, u32[]{:S(2)}) collective-permute-start(bf16[16,128,256]{2,1,0:T(8,128)(2,1)S(1)} %convolution_convert_fusion.3), channel_id=1, source_target_pairs={{0,1},{1,0},{2,3},{3,2},{4,5},{5,4},{6,7},{7,6},{8,9},{9,8},{10,11... | collective-permute-start | bytes 3145736 | tf_op jit(solution)/shard_map/ppermute | solution.py:28
  478.9 317.5 %all-gather.23.cloned.1.call-start = ((), (), s32[]{:S(2)}) async-start(), calls=%async_computation.7 | async-start | bytes 5242880 | tf_op jit(solution)/shard_map/all_gather | solution.py:178
  497.9 29.8 %collective-permute-start.22 = (bf16[16,128,256]{2,1,0:T(8,128)(2,1)}, bf16[16,128,256]{2,1,0:T(8,128)(2,1)}, u32[]{:S(2)}, u32[]{:S(2)}) collective-permute-start(bf16[16,128,256]{2,1,0:T(8,128)(2,1)} %convolution_convert_fusion.2), channel_id=1, source_target_pairs={{0,1},{1,0},{2,3},{3,2},{4,5},{5,4},{6,7},{7,6},{8,9},{9,8},{10,11... | collective-permute-start | bytes 3145736 | tf_op jit(solution)/shard_map/ppermute | solution.py:28
  532.8 24.3 %collective-permute-start.23 = (bf16[16,128,256]{2,1,0:T(8,128)(2,1)S(1)}, bf16[16,128,256]{2,1,0:T(8,128)(2,1)S(1)}, u32[]{:S(2)}, u32[]{:S(2)}) collective-permute-start(bf16[16,128,256]{2,1,0:T(8,128)(2,1)S(1)} %convolution_convert_fusion.1), channel_id=1, source_target_pairs={{0,1},{1,0},{2,3},{3,2},{4,5},{5,4},{6,7},{7,6},{8,9},{9,8},{10,11... | collective-permute-start | bytes 3145736 | tf_op jit(solution)/shard_map/ppermute | solution.py:28
  580.5 215.9 %all-gather.21.cloned.1.call-start = ((), (), s32[]{:S(2)}) async-start(), calls=%async_computation.6 | async-start | bytes 5242880 | tf_op jit(solution)/shard_map/all_gather | solution.py:178
  581.1 395.1 %all-gather.19.cloned.1.call-start = ((), (), s32[]{:S(2)}) async-start(), calls=%async_computation.5 | async-start | bytes 5242880 | tf_op jit(solution)/shard_map/all_gather | solution.py:178
  585.1 23.3 %collective-permute-start.25 = (bf16[16,128,256]{2,1,0:T(8,128)(2,1)}, bf16[16,128,256]{2,1,0:T(8,128)(2,1)}, u32[]{:S(2)}, u32[]{:S(2)}) collective-permute-start(bf16[16,128,256]{2,1,0:T(8,128)(2,1)} %convolution_convert_fusion), channel_id=1, source_target_pairs={{0,1},{1,0},{2,3},{3,2},{4,5},{5,4},{6,7},{7,6},{8,9},{9,8},{10,11... | collective-permute-start | bytes 3145736 | tf_op jit(solution)/shard_map/ppermute | solution.py:28
  613.8 362.3 %all-gather.15.cloned.1.call-start = ((), (), s32[]{:S(2)}) async-start(), calls=%async_computation.3 | async-start | bytes 5242880 | tf_op jit(solution)/shard_map/all_gather | solution.py:178
  614.6 91.9 %collective-permute-start.28 = (bf16[4,16,128,256]{3,2,1,0:T(8,128)(2,1)}, bf16[4,16,128,256]{3,2,1,0:T(8,128)(2,1)}, u32[]{:S(2)}, u32[]{:S(2)}) collective-permute-start(bf16[4,16,128,256]{3,2,1,0:T(8,128)(2,1)} %all-gather.11.cloned.1.call-done.refs_5_.refs_2_), channel_id=1, source_target_pairs={{0,1},{1,0},{2,3},{3,2},{4,5},{5,4},{6,7},{7,6},{8,9},{9,8},{10,11... | collective-permute-start | bytes 12582920 | tf_op jit(solution)/shard_map/ppermute | solution.py:28
  615.8 180.6 %collective-permute-start.29 = (bf16[4,16,128,256]{3,2,1,0:T(8,128)(2,1)}, bf16[4,16,128,256]{3,2,1,0:T(8,128)(2,1)}, u32[]{:S(2)}, u32[]{:S(2)}) collective-permute-start(bf16[4,16,128,256]{3,2,1,0:T(8,128)(2,1)} %all-gather.17.cloned.1.call-done.refs_5_.refs_3_), channel_id=1, source_target_pairs={{0,1},{1,0},{2,3},{3,2},{4,5},{5,4},{6,7},{7,6},{8,9},{9,8},{10,11... | collective-permute-start | bytes 12582920 | tf_op jit(solution)/shard_map/ppermute | solution.py:28
  616.1 270.1 %collective-permute-start.26 = (bf16[4,16,128,256]{3,2,1,0:T(8,128)(2,1)}, bf16[4,16,128,256]{3,2,1,0:T(8,128)(2,1)}, u32[]{:S(2)}, u32[]{:S(2)}) collective-permute-start(bf16[4,16,128,256]{3,2,1,0:T(8,128)(2,1)} %all-gather.9.cloned.1.call-done.refs_5_.refs_2_), channel_id=1, source_target_pairs={{0,1},{1,0},{2,3},{3,2},{4,5},{5,4},{6,7},{7,6},{8,9},{9,8},{10,11... | collective-permute-start | bytes 12582920 | tf_op jit(solution)/shard_map/ppermute | solution.py:28
  617.3 358.9 %collective-permute-start.27 = (bf16[4,16,128,256]{3,2,1,0:T(8,128)(2,1)}, bf16[4,16,128,256]{3,2,1,0:T(8,128)(2,1)}, u32[]{:S(2)}, u32[]{:S(2)}) collective-permute-start(bf16[4,16,128,256]{3,2,1,0:T(8,128)(2,1)} %all-gather.13.cloned.1.call-done.refs_5_.refs_3_), channel_id=1, source_target_pairs={{0,1},{1,0},{2,3},{3,2},{4,5},{5,4},{6,7},{7,6},{8,9},{9,8},{10,11... | collective-permute-start | bytes 12582920 | tf_op jit(solution)/shard_map/ppermute | solution.py:28
  (54 other events, 708.0 us)
Sparse Core Ops, SparseCore 0:
  269.8 82.7 all-gather.8
  354.2 79.2 all-gather.10
  435.0 79.2 all-gather.12
  515.8 79.2 all-gather.16
  596.5 79.3 all-gather.22
  677.4 79.3 all-gather.20
  758.9 79.2 all-gather.18
  839.8 79.2 all-gather.14

commit v3 on v2

--- a/solution.py
+++ b/solution.py
@@ -23,9 +23,12 @@
     return local, remote
 
 
-def swapped(block, distance):
+def swapped(block, distance, pipes=None):
     count = lax.axis_size("tensor")
-    return lax.ppermute(block, "tensor", [(i, i ^ distance) for i in range(count)])
+    if pipes is None:
+        pipes = range(lax.axis_size("pipe"))
+    pairs = [(p * count + i, p * count + (i ^ distance)) for p in pipes for i in range(count)]
+    return lax.ppermute(block, ("pipe", "tensor"), pairs)
 
 
 def passed_along(x, by):
@@ -137,8 +140,11 @@
     inputs = to_blocks(inputs)
     cotangent = to_blocks(cotangent)
 
-    def apply_forward(v, w):
-        partners = [swapped(v, d) for _, d in remote]
+    def working(step, sections_in_order):
+        return [p for pos, p in enumerate(sections_in_order) if 0 <= step - pos < micro]
+
+    def apply_forward(v, w, pipes):
+        partners = [swapped(v, d, pipes) for _, d in remote]
         total = local_apply(v, w, local, False)
         for (k, _), partner in zip(remote, partners):
             total = total + jnp.einsum(
@@ -146,11 +152,11 @@
             )
         return total
 
-    def apply_transposed(g, w, after=()):
+    def apply_transposed(g, w, pipes, after=()):
         sent = []
         for k, d in remote:
             term = jnp.einsum("ltc,lbc->ltb", g, w[:, k], preferred_element_type=jnp.float32)
-            sent.append(swapped(term.astype(jnp.bfloat16), d))
+            sent.append(swapped(term.astype(jnp.bfloat16), d, pipes))
         total = local_apply(g, w, local, True, after)
         for term in sent:
             total = total + term.astype(jnp.float32)
@@ -164,11 +170,14 @@
             layer_in = own
         else:
             layer_in = jnp.where(segment == 0, own, passed_along(outgoing, 1))
-        hidden = apply_forward(layer_in, w_up)
+        pipes = working(step, range(sections))
+        hidden = apply_forward(layer_in, w_up, pipes)
         act = gelu_value(hidden).astype(jnp.bfloat16)
-        mixed = apply_forward(act, w_down)
-        outgoing = (layer_in.astype(jnp.float32) + mixed).astype(jnp.bfloat16)
         kept.append((layer_in, act, hidden))
+        if step < steps - 1:
+            onward = [p for p in pipes if p < sections - 1]
+            mixed = apply_forward(act, w_down, onward)
+            outgoing = (layer_in.astype(jnp.float32) + mixed).astype(jnp.bfloat16)
 
     def own_step(items, first, m):
         window = items[m : m + sections]
@@ -182,7 +191,12 @@
         z_all.append(gathered(own_step([x[0] for x in kept], segment, m)))
         act_all.append(gathered(own_step([x[1] for x in kept], segment, m)))
     hidden = jnp.stack([own_step([x[2] for x in kept], segment, m) for m in range(micro)])
-    due = [x for pair in zip(z_all, act_all) for x in pair]
+    due = {}
+    for pos, x in enumerate([x for pair in zip(z_all, act_all) for x in pair]):
+        due.setdefault(3 * pos, []).append(x)
+    z_partners = [[swapped(x, d) for x in z_all] for _, d in remote]
+    act_partners = [[swapped(x, d) for x in act_all] for _, d in remote]
+    due.setdefault(2 * steps - 2, []).extend(group[0] for group in z_partners)
 
     made = []
     for step in range(steps):
@@ -192,15 +206,15 @@
             grads = own
         else:
             grads = jnp.where(segment == sections - 1, own, passed_along(outgoing, -1))
-        after = due[step - 1 : step] if step < steps - 1 else due[step - 1 :]
-        grad_act = apply_transposed(grads, w_down, after if step else ())
+        pipes = working(step, range(sections - 1, -1, -1))
+        grad_act = apply_transposed(grads, w_down, pipes, due.get(2 * step, ()))
         slope = gelu_slope(lax.dynamic_index_in_dim(hidden, index, 0, keepdims=False))
         grad_hidden = (grad_act * slope).astype(jnp.bfloat16)
         made.append((grads, grad_hidden))
         if step < steps - 1:
-            outgoing = (
-                grads.astype(jnp.float32) + apply_transposed(grad_hidden, w_up)
-            ).astype(jnp.bfloat16)
+            onward = [p for p in pipes if p > 0]
+            passed = apply_transposed(grad_hidden, w_up, onward, due.get(2 * step + 1, ()))
+            outgoing = (grads.astype(jnp.float32) + passed).astype(jnp.bfloat16)
 
     g_all, grad_hidden_all = [], []
     last = sections - 1 - segment
@@ -208,8 +222,6 @@
         g_all.append(gathered(own_step([x[0] for x in made], last, m)))
         grad_hidden_all.append(gathered(own_step([x[1] for x in made], last, m)))
 
-    act_partners = [[swapped(x, d) for x in act_all] for _, d in remote]
-    z_partners = [[swapped(x, d) for x in z_all] for _, d in remote]
     grad_down = weight_grad(act_all, g_all, act_partners, local, remote)
     grad_up = weight_grad(z_all, grad_hidden_all, z_partners, local, remote)
     return grad_up[None], grad_down[None]

time: 1030 us -> 989 us (0.960)
  waiting for transfers between devices: 545 us -> 492 us
  starting transfers between devices: 60.1 us -> 73.5 us
    ppermute x22, waiting for transfers between devices: 398 us -> 334 us  [swapped(): return lax.ppermute(block, ('pipe', 'tensor'), pairs)]
    ppermute x22, starting transfers between devices: 22.3 us -> 38.3 us  [swapped(): return lax.ppermute(block, ('pipe', 'tensor'), pairs)]
    all_gather x8, waiting for transfers between devices: 36.7 us -> 51.9 us  [gathered(): return lax.all_gather(x, 'dp')]
  transfers between devices with their start and end apart: 38 -> 38, of which waited for: 27 -> 19; matrix products, arithmetic and copies ran while one was open for 7% -> 7% of each run, Pallas kernels for 25% -> 26%
where the time goes in v3:
time: 989 us; the launch traced here: 975 us
  waiting for transfers between devices  492 us (50%)
  Pallas kernels  275 us (28%)
  starting transfers between devices  73.5 us (7%)
  matrix products  48.2 us (5%)
  other arithmetic  46.8 us (5%)
  local copies, waits for them, and re-layouts  23.1 us (2%)
  between operations  15.7 us (2%)
    ppermute x22, waiting for transfers between devices, swapped(): return lax.ppermute(block, ('pipe', 'tensor'), pairs)  334 us
    pallas_call x18, Pallas kernels, local_apply(): pl.pallas_call(functools.partial(apply_body, local, transpose), out_shape...  223 us
    ppermute x8, waiting for transfers between devices, passed_along(): lax.ppermute(x, 'pipe', [(i, i + by) for i in range(size) if 0 <= i + by...  104 us
    pallas_call x2, Pallas kernels, weight_grad(): pl.pallas_call(functools.partial(grad_body, local, remote, micro), out_sh...  52.8 us
    all_gather x8, waiting for transfers between devices, gathered(): return lax.all_gather(x, 'dp')  51.9 us
    ppermute x22, starting transfers between devices, swapped(): return lax.ppermute(block, ('pipe', 'tensor'), pairs)  38.3 us
    ppermute x8, starting transfers between devices, passed_along(): lax.ppermute(x, 'pipe', [(i, i + by) for i in range(size) if 0 <= i + by...  34.6 us
    dot_general x9, matrix products, apply_transposed(): jnp.einsum('ltc,lbc->ltb', g, w[:, k], preferred_element_type=jnp.float32)  28.3 us
  transfers between devices with their start and end apart: 38, of which 19 were waited for; matrix products, arithmetic and copies ran while one was open for 7% of the time, Pallas kernels for 26%

profile of v3, /device:TPU:1, one launch (start us, length us, event | category | flops | bytes accessed | tf_op | source)
XLA Modules:
  0.0 974.5 jit_solution(8141211424380359980)
XLA Ops:
  32.5 11.7 %shard_map.60 = f32[16,128,256]{2,1,0:T(8,128)S(1)} custom-call(bf16[16,128,256]{2,1,0:T(8,128)(2,1)S(1)} %get-tuple-element.24.v_ref, bf16[16,6,256,256]{3,2,1,0:T(8,128)(2,1)} %bitcast.198, bf16[16,6,256,256]{3,2,1,0:T(8,128)(2,1)} %bitcast.199, bf16[16,6,256,256]{3,2,1,0:T(8,128)(2,1)} %bitcast.200, bf16[16,6,256,256]{3,2,1,0:T(8,128)(2,1)} %bitcast.201, ...), custom_call_target="tpu_custom_call" | custom-call | flops 1342177280 | bytes 13631488 | tf_op jit(solution)/shard_map/pallas_call | solution.py:64
  220.7 12.6 %collective-permute-start.12 = (bf16[16,128,256]{2,1,0:T(8,128)(2,1)}, bf16[16,128,256]{2,1,0:T(8,128)(2,1)}, u32[]{:S(2)}, u32[]{:S(2)}) collective-permute-start(bf16[16,128,256]{2,1,0:T(8,128)(2,1)} %add_convert_fusion.4), channel_id=1, source_target_pairs={{0,2},{2,4},{4,6},{1,3},{3,5},{5,7},{8,10},{10,12},{12,14},{9,11},... | collective-permute-start | bytes 3145736 | tf_op jit(solution)/shard_map/ppermute | solution.py:36
  233.3 12.0 %collective-permute-done.12 = bf16[16,128,256]{2,1,0:T(8,128)(2,1)} collective-permute-done((bf16[16,128,256]{2,1,0:T(8,128)(2,1)}, bf16[16,128,256]{2,1,0:T(8,128)(2,1)}, u32[]{:S(2)}, u32[]{:S(2)}) %collective-permute-start.12) | collective-permute-done | bytes 1048608 | tf_op jit(solution)/shard_map/ppermute | solution.py:36
  263.7 11.7 %shard_map.68 = f32[16,128,256]{2,1,0:T(8,128)S(1)} custom-call(bf16[16,128,256]{2,1,0:T(8,128)(2,1)S(1)} %copy-done.17, bf16[16,6,256,256]{3,2,1,0:T(8,128)(2,1)} %bitcast.170, bf16[16,6,256,256]{3,2,1,0:T(8,128)(2,1)} %bitcast.169, bf16[16,6,256,256]{3,2,1,0:T(8,128)(2,1)} %bitcast.168, bf16[16,6,256,256]{3,2,1,0:T(8,128)(2,1)} %bitcast.171, ...), custom_call_target="tpu_custom_call" | custom-call | flops 1342177280 | bytes 13631488 | tf_op jit(solution)/shard_map/pallas_call | solution.py:64
  290.1 43.2 %all-gather.9.cloned.1.call-done.refs_5_.refs_2_ = bf16[4,16,128,256]{3,2,1,0:T(8,128)(2,1)} async-done(((bf16[1,16,128,256]{3,2,1,0:T(8,128)(2,1)}), bf16[4,16,128,256]{3,2,1,0:T(8,128)(2,1)}) %all-gather.9.cloned.1.call-update) | async-done | bytes 4194320 | tf_op jit(solution)/shard_map/all_gather | solution.py:187
  333.4 13.2 %shard_map.65 = f32[16,128,256]{2,1,0:T(8,128)S(1)} custom-call(bf16[16,128,256]{2,1,0:T(8,128)(2,1)S(1)} %get-tuple-element.21.v_ref, bf16[16,6,256,256]{3,2,1,0:T(8,128)(2,1)} %bitcast.224, bf16[16,6,256,256]{3,2,1,0:T(8,128)(2,1)} %bitcast.223, bf16[16,6,256,256]{3,2,1,0:T(8,128)(2,1)} %bitcast.225, bf16[16,6,256,256]{3,2,1,0:T(8,128)(2,1)} %bitcast.226, ...), custom_call_target="tpu_custom_call" | custom-call | flops 1342177280 | bytes 13631488 | tf_op jit(solution)/shard_map/pallas_call | solution.py:64
  352.6 12.8 %shard_map.69 = f32[16,128,256]{2,1,0:T(8,128)S(1)} custom-call(bf16[16,128,256]{2,1,0:T(8,128)(2,1)S(1)} %fusion.4.v_ref, bf16[16,6,256,256]{3,2,1,0:T(8,128)(2,1)} %bitcast.175, bf16[16,6,256,256]{3,2,1,0:T(8,128)(2,1)} %bitcast.176, bf16[16,6,256,256]{3,2,1,0:T(8,128)(2,1)} %bitcast.177, bf16[16,6,256,256]{3,2,1,0:T(8,128)(2,1)} %bitcast.178, ...), custom_call_target="tpu_custom_call" | custom-call | flops 1342177280 | bytes 13631488 | tf_op jit(solution)/shard_map/pallas_call | solution.py:64
  368.7 13.8 %collective-permute-done.15 = bf16[16,128,256]{2,1,0:T(8,128)(2,1)} collective-permute-done((bf16[16,128,256]{2,1,0:T(8,128)(2,1)S(1)}, bf16[16,128,256]{2,1,0:T(8,128)(2,1)}, u32[]{:S(2)}, u32[]{:S(2)}) %collective-permute-start.15) | collective-permute-done | bytes 1048608 | tf_op jit(solution)/shard_map/ppermute | solution.py:36
  387.0 13.0 %shard_map.70 = f32[16,128,256]{2,1,0:T(8,128)S(1)} custom-call(bf16[16,128,256]{2,1,0:T(8,128)(2,1)S(1)} %broadcast_select_fusion.3.v_ref, bf16[16,6,256,256]{3,2,1,0:T(8,128)(2,1)} %bitcast.229, bf16[16,6,256,256]{3,2,1,0:T(8,128)(2,1)} %bitcast.230, bf16[16,6,256,256]{3,2,1,0:T(8,128)(2,1)} %bitcast.231, bf16[16,6,256,256]{3,2,1,0:T(8,128)(2,1)} %bitcast.232, ...), custom_call_target="tpu_custom_call" | custom-call | flops 1342177280 | bytes 13631488 | tf_op jit(solution)/shard_map/pallas_call | solution.py:64
  414.6 13.1 %shard_map.71 = f32[16,128,256]{2,1,0:T(8,128)S(1)} custom-call(bf16[16,128,256]{2,1,0:T(8,128)(2,1)S(1)} %fusion.9.v_ref, bf16[16,6,256,256]{3,2,1,0:T(8,128)(2,1)} %bitcast.183, bf16[16,6,256,256]{3,2,1,0:T(8,128)(2,1)} %bitcast.182, bf16[16,6,256,256]{3,2,1,0:T(8,128)(2,1)} %bitcast.181, bf16[16,6,256,256]{3,2,1,0:T(8,128)(2,1)} %bitcast.184, ...), custom_call_target="tpu_custom_call" | custom-call | flops 1342177280 | bytes 13631488 | tf_op jit(solution)/shard_map/pallas_call | solution.py:64
  430.7 14.2 %collective-permute-done.18 = bf16[16,128,256]{2,1,0:T(8,128)(2,1)S(1)} collective-permute-done((bf16[16,128,256]{2,1,0:T(8,128)(2,1)S(1)}, bf16[16,128,256]{2,1,0:T(8,128)(2,1)S(1)}, u32[]{:S(2)}, u32[]{:S(2)}) %collective-permute-start.18) | collective-permute-done | bytes 1048608 | tf_op jit(solution)/shard_map/ppermute | solution.py:36
  451.5 13.0 %shard_map.72 = f32[16,128,256]{2,1,0:T(8,128)S(1)} custom-call(bf16[16,128,256]{2,1,0:T(8,128)(2,1)S(1)} %broadcast_select_fusion.2.v_ref, bf16[16,6,256,256]{3,2,1,0:T(8,128)(2,1)} %bitcast.238, bf16[16,6,256,256]{3,2,1,0:T(8,128)(2,1)} %bitcast.236, bf16[16,6,256,256]{3,2,1,0:T(8,128)(2,1)} %bitcast.237, bf16[16,6,256,256]{3,2,1,0:T(8,128)(2,1)} %bitcast.235, ...), custom_call_target="tpu_custom_call" | custom-call | flops 1342177280 | bytes 13631488 | tf_op jit(solution)/shard_map/pallas_call | solution.py:64
  471.7 12.8 %shard_map.73 = f32[16,128,256]{2,1,0:T(8,128)S(1)} custom-call(bf16[16,128,256]{2,1,0:T(8,128)(2,1)S(1)} %fusion.14.v_ref, bf16[16,6,256,256]{3,2,1,0:T(8,128)(2,1)} %bitcast.187, bf16[16,6,256,256]{3,2,1,0:T(8,128)(2,1)} %bitcast.188, bf16[16,6,256,256]{3,2,1,0:T(8,128)(2,1)} %bitcast.189, bf16[16,6,256,256]{3,2,1,0:T(8,128)(2,1)} %bitcast.190, ...), custom_call_target="tpu_custom_call" | custom-call | flops 1342177280 | bytes 13631488 | tf_op jit(solution)/shard_map/pallas_call | solution.py:64
  487.0 14.5 %collective-permute-done.21 = bf16[16,128,256]{2,1,0:T(8,128)(2,1)} collective-permute-done((bf16[16,128,256]{2,1,0:T(8,128)(2,1)S(1)}, bf16[16,128,256]{2,1,0:T(8,128)(2,1)}, u32[]{:S(2)}, u32[]{:S(2)}) %collective-permute-start.21) | collective-permute-done | bytes 1048608 | tf_op jit(solution)/shard_map/ppermute | solution.py:36
  510.1 13.0 %shard_map.74 = f32[16,128,256]{2,1,0:T(8,128)S(1)} custom-call(bf16[16,128,256]{2,1,0:T(8,128)(2,1)S(1)} %broadcast_select_fusion.1.v_ref, bf16[16,6,256,256]{3,2,1,0:T(8,128)(2,1)} %bitcast.241, bf16[16,6,256,256]{3,2,1,0:T(8,128)(2,1)} %bitcast.242, bf16[16,6,256,256]{3,2,1,0:T(8,128)(2,1)} %bitcast.243, bf16[16,6,256,256]{3,2,1,0:T(8,128)(2,1)} %bitcast.244, ...), custom_call_target="tpu_custom_call" | custom-call | flops 1342177280 | bytes 13631488 | tf_op jit(solution)/shard_map/pallas_call | solution.py:64
  531.3 12.9 %shard_map.75 = f32[16,128,256]{2,1,0:T(8,128)S(1)} custom-call(bf16[16,128,256]{2,1,0:T(8,128)(2,1)S(1)} %fusion.19.v_ref, bf16[16,6,256,256]{3,2,1,0:T(8,128)(2,1)} %bitcast.193, bf16[16,6,256,256]{3,2,1,0:T(8,128)(2,1)} %bitcast.194, bf16[16,6,256,256]{3,2,1,0:T(8,128)(2,1)} %bitcast.195, bf16[16,6,256,256]{3,2,1,0:T(8,128)(2,1)} %bitcast.196, ...), custom_call_target="tpu_custom_call" | custom-call | flops 1342177280 | bytes 13631488 | tf_op jit(solution)/shard_map/pallas_call | solution.py:64
  547.6 14.8 %collective-permute-done.24 = bf16[16,128,256]{2,1,0:T(8,128)(2,1)} collective-permute-done((bf16[16,128,256]{2,1,0:T(8,128)(2,1)}, bf16[16,128,256]{2,1,0:T(8,128)(2,1)}, u32[]{:S(2)}, u32[]{:S(2)}) %collective-permute-start.24) | collective-permute-done | bytes 1048608 | tf_op jit(solution)/shard_map/ppermute | solution.py:36
  572.2 88.3 %collective-permute-done.25.refs_5_.refs_4_ = bf16[4,16,128,256]{3,2,1,0:T(8,128)(2,1)} collective-permute-done((bf16[4,16,128,256]{3,2,1,0:T(8,128)(2,1)}, bf16[4,16,128,256]{3,2,1,0:T(8,128)(2,1)}, u32[]{:S(2)}, u32[]{:S(2)}) %collective-permute-start.25) | collective-permute-done | bytes 4194336 | tf_op jit(solution)/shard_map/ppermute | solution.py:31
  660.4 13.0 %shard_map.76 = f32[16,128,256]{2,1,0:T(8,128)S(1)} custom-call(bf16[16,128,256]{2,1,0:T(8,128)(2,1)S(1)} %copy-done.9, bf16[16,6,256,256]{3,2,1,0:T(8,128)(2,1)} %bitcast.247, bf16[16,6,256,256]{3,2,1,0:T(8,128)(2,1)} %bitcast.248, bf16[16,6,256,256]{3,2,1,0:T(8,128)(2,1)} %bitcast.249, bf16[16,6,256,256]{3,2,1,0:T(8,128)(2,1)} %bitcast.250, ...), custom_call_target="tpu_custom_call" | custom-call | flops 1342177280 | bytes 13631488 | tf_op jit(solution)/shard_map/pallas_call | solution.py:64
  682.0 90.3 %collective-permute-done.28.refs_4_ = bf16[4,16,128,256]{3,2,1,0:T(8,128)(2,1)} collective-permute-done((bf16[4,16,128,256]{3,2,1,0:T(8,128)(2,1)}, bf16[4,16,128,256]{3,2,1,0:T(8,128)(2,1)}, u32[]{:S(2)}, u32[]{:S(2)}) %collective-permute-start.28) | collective-permute-done | bytes 4194336 | tf_op jit(solution)/shard_map/ppermute | solution.py:31
  772.3 89.9 %collective-permute-done.29.refs_5_ = bf16[4,16,128,256]{3,2,1,0:T(8,128)(2,1)} collective-permute-done((bf16[4,16,128,256]{3,2,1,0:T(8,128)(2,1)}, bf16[4,16,128,256]{3,2,1,0:T(8,128)(2,1)}, u32[]{:S(2)}, u32[]{:S(2)}) %collective-permute-start.29) | collective-permute-done | bytes 4194336 | tf_op jit(solution)/shard_map/ppermute | solution.py:31
  864.4 26.4 %shard_map.78 = f32[16,6,256,256]{3,2,1,0:T(8,128)} custom-call(bf16[4,16,128,256]{3,2,1,0:T(8,128)(2,1)S(1)} %copy-done.20, bf16[4,16,128,256]{3,2,1,0:T(8,128)(2,1)} %all-gather.21.cloned.1.call-done.refs_1_, bf16[4,16,128,256]{3,2,1,0:T(8,128)(2,1)} %all-gather.11.cloned.1.call-done.refs_5_.refs_2_, ...), custom_call_target="tpu_custom_call" | custom-call | flops 12884901888 | bytes 41943040 | tf_op jit(solution)/shard_map/pallas_call | solution.py:112
  890.8 47.9 %collective-permute-done.27.refs_5_ = bf16[4,16,128,256]{3,2,1,0:T(8,128)(2,1)} collective-permute-done((bf16[4,16,128,256]{3,2,1,0:T(8,128)(2,1)}, bf16[4,16,128,256]{3,2,1,0:T(8,128)(2,1)}, u32[]{:S(2)}, u32[]{:S(2)}) %collective-permute-start.27) | collective-permute-done | bytes 4194336 | tf_op jit(solution)/shard_map/ppermute | solution.py:31
  940.9 26.4 %shard_map.77 = f32[16,6,256,256]{3,2,1,0:T(8,128)} custom-call(bf16[4,16,128,256]{3,2,1,0:T(8,128)(2,1)S(1)} %copy-done.21, bf16[4,16,128,256]{3,2,1,0:T(8,128)(2,1)} %all-gather.17.cloned.1.call-done.refs_1_, bf16[4,16,128,256]{3,2,1,0:T(8,128)(2,1)} %all-gather.9.cloned.1.call-done.refs_5_.refs_2_, ...), custom_call_target="tpu_custom_call" | custom-call | flops 12884901888 | bytes 41943040 | tf_op jit(solution)/shard_map/pallas_call | solution.py:112
  (212 shorter events, 324.2 us)
Async XLA Ops:
  7.2 326.2 %all-gather.9.cloned.1.call-start = ((), (), s32[]{:S(2)}) async-start(), calls=%async_computation | async-start | bytes 5242880 | tf_op jit(solution)/shard_map/all_gather | solution.py:187
  64.4 22.9 %collective-permute-start.3 = (bf16[16,128,256]{2,1,0:T(8,128)(2,1)S(1)}, bf16[16,128,256]{2,1,0:T(8,128)(2,1)S(1)}, u32[]{:S(2)}, u32[]{:S(2)}) collective-permute-start(bf16[16,128,256]{2,1,0:T(8,128)(2,1)S(1)} %broadcast_select_fusion.7.v_ref), channel_id=1, source_target_pairs={{0,1},{1,0},{2,3},{3,2},{8,9},{9,8},{10,11},{11,10},{16,17},{17,16... | collective-permute-start | bytes 3145736 | tf_op jit(solution)/shard_map/ppermute | solution.py:31
  91.2 24.4 %collective-permute-start.4 = (bf16[16,128,256]{2,1,0:T(8,128)(2,1)S(1)}, bf16[16,128,256]{2,1,0:T(8,128)(2,1)S(1)}, u32[]{:S(2)}, u32[]{:S(2)}) collective-permute-start(bf16[16,128,256]{2,1,0:T(8,128)(2,1)S(1)} %get-tuple-element.10.v_ref), channel_id=1, source_target_pairs={{0,1},{1,0},{2,3},{3,2},{8,9},{9,8},{10,11},{11,10},{16,17},{17,16... | collective-permute-start | bytes 3145736 | tf_op jit(solution)/shard_map/ppermute | solution.py:31
  169.9 18.1 %collective-permute-start.8 = (bf16[16,128,256]{2,1,0:T(8,128)(2,1)S(1)}, bf16[16,128,256]{2,1,0:T(8,128)(2,1)S(1)}, u32[]{:S(2)}, u32[]{:S(2)}) collective-permute-start(bf16[16,128,256]{2,1,0:T(8,128)(2,1)S(1)} %add_convert_fusion.5), channel_id=1, source_target_pairs={{0,2},{2,4},{4,6},{1,3},{3,5},{5,7},{8,10},{10,12},{12,14},{9,11},... | collective-permute-start | bytes 3145736 | tf_op jit(solution)/shard_map/ppermute | solution.py:36
  220.7 24.6 %collective-permute-start.12 = (bf16[16,128,256]{2,1,0:T(8,128)(2,1)}, bf16[16,128,256]{2,1,0:T(8,128)(2,1)}, u32[]{:S(2)}, u32[]{:S(2)}) collective-permute-start(bf16[16,128,256]{2,1,0:T(8,128)(2,1)} %add_convert_fusion.4), channel_id=1, source_target_pairs={{0,2},{2,4},{4,6},{1,3},{3,5},{5,7},{8,10},{10,12},{12,14},{9,11},... | collective-permute-start | bytes 3145736 | tf_op jit(solution)/shard_map/ppermute | solution.py:36
  250.0 164.6 %all-gather.11.cloned.1.call-start = ((), (), s32[]{:S(2)}) async-start(), calls=%async_computation.1 | async-start | bytes 5242880 | tf_op jit(solution)/shard_map/all_gather | solution.py:187
  250.0 25.4 %collective-permute-start.13 = (bf16[16,128,256]{2,1,0:T(8,128)(2,1)}, bf16[16,128,256]{2,1,0:T(8,128)(2,1)S(1)}, u32[]{:S(2)}, u32[]{:S(2)}) collective-permute-start(bf16[16,128,256]{2,1,0:T(8,128)(2,1)} %copy-done.16), channel_id=1, source_target_pairs={{6,7},{7,6},{14,15},{15,14},{22,23},{23,22},{30,31},{31,30}} | collective-permute-start | bytes 3145736 | tf_op jit(solution)/shard_map/ppermute | solution.py:31
  262.0 84.6 %collective-permute-start.9 = (bf16[16,128,256]{2,1,0:T(8,128)(2,1)}, bf16[16,128,256]{2,1,0:T(8,128)(2,1)}, u32[]{:S(2)}, u32[]{:S(2)}) collective-permute-start(bf16[16,128,256]{2,1,0:T(8,128)(2,1)} %convolution_convert_fusion.8), channel_id=1, source_target_pairs={{6,7},{7,6},{14,15},{15,14},{22,23},{23,22},{30,31},{31,30}} | collective-permute-start | bytes 3145736 | tf_op jit(solution)/shard_map/ppermute | solution.py:31
  283.4 226.7 %all-gather.13.cloned.1.call-start = ((), (), s32[]{:S(2)}) async-start(), calls=%async_computation.2 | async-start | bytes 5242880 | tf_op jit(solution)/shard_map/all_gather | solution.py:187
  366.0 16.6 %collective-permute-start.15 = (bf16[16,128,256]{2,1,0:T(8,128)(2,1)S(1)}, bf16[16,128,256]{2,1,0:T(8,128)(2,1)}, u32[]{:S(2)}, u32[]{:S(2)}) collective-permute-start(bf16[16,128,256]{2,1,0:T(8,128)(2,1)S(1)} %add_convert_fusion.3), channel_id=1, source_target_pairs={{2,0},{4,2},{6,4},{3,1},{5,3},{7,5},{10,8},{12,10},{14,12},{11,9},... | collective-permute-start | bytes 3145736 | tf_op jit(solution)/shard_map/ppermute | solution.py:36
  405.2 22.5 %collective-permute-start.17 = (bf16[16,128,256]{2,1,0:T(8,128)(2,1)}, bf16[16,128,256]{2,1,0:T(8,128)(2,1)S(1)}, u32[]{:S(2)}, u32[]{:S(2)}) collective-permute-start(bf16[16,128,256]{2,1,0:T(8,128)(2,1)} %convolution_convert_fusion.5), channel_id=1, source_target_pairs={{6,7},{7,6},{4,5},{5,4},{14,15},{15,14},{12,13},{13,12},{22,23},{2... | collective-permute-start | bytes 3145736 | tf_op jit(solution)/shard_map/ppermute | solution.py:31
  405.9 274.6 %all-gather.23.cloned.1.call-start = ((), (), s32[]{:S(2)}) async-start(), calls=%async_computation.7 | async-start | bytes 5242880 | tf_op jit(solution)/shard_map/all_gather | solution.py:187
  428.2 16.6 %collective-permute-start.18 = (bf16[16,128,256]{2,1,0:T(8,128)(2,1)S(1)}, bf16[16,128,256]{2,1,0:T(8,128)(2,1)S(1)}, u32[]{:S(2)}, u32[]{:S(2)}) collective-permute-start(bf16[16,128,256]{2,1,0:T(8,128)(2,1)S(1)} %add_convert_fusion.2), channel_id=1, source_target_pairs={{2,0},{4,2},{6,4},{3,1},{5,3},{7,5},{10,8},{12,10},{14,12},{11,9},... | collective-permute-start | bytes 3145736 | tf_op jit(solution)/shard_map/ppermute | solution.py:36
  485.0 16.5 %collective-permute-start.21 = (bf16[16,128,256]{2,1,0:T(8,128)(2,1)S(1)}, bf16[16,128,256]{2,1,0:T(8,128)(2,1)}, u32[]{:S(2)}, u32[]{:S(2)}) collective-permute-start(bf16[16,128,256]{2,1,0:T(8,128)(2,1)S(1)} %add_convert_fusion.1), channel_id=1, source_target_pairs={{2,0},{4,2},{6,4},{3,1},{5,3},{7,5},{10,8},{12,10},{14,12},{11,9},... | collective-permute-start | bytes 3145736 | tf_op jit(solution)/shard_map/ppermute | solution.py:36
  487.0 375.2 %all-gather.21.cloned.1.call-start = ((), (), s32[]{:S(2)}) async-start(), calls=%async_computation.6 | async-start | bytes 5242880 | tf_op jit(solution)/shard_map/all_gather | solution.py:187
  545.7 16.7 %collective-permute-start.24 = (bf16[16,128,256]{2,1,0:T(8,128)(2,1)}, bf16[16,128,256]{2,1,0:T(8,128)(2,1)}, u32[]{:S(2)}, u32[]{:S(2)}) collective-permute-start(bf16[16,128,256]{2,1,0:T(8,128)(2,1)} %add_convert_fusion), channel_id=1, source_target_pairs={{2,0},{4,2},{6,4},{3,1},{5,3},{7,5},{10,8},{12,10},{14,12},{11,9},... | collective-permute-start | bytes 3145736 | tf_op jit(solution)/shard_map/ppermute | solution.py:36
  566.9 295.2 %all-gather.19.cloned.1.call-start = ((), (), s32[]{:S(2)}) async-start(), calls=%async_computation.5 | async-start | bytes 5242880 | tf_op jit(solution)/shard_map/all_gather | solution.py:187
  567.5 371.2 %all-gather.17.cloned.1.call-start = ((), (), s32[]{:S(2)}) async-start(), calls=%async_computation.4 | async-start | bytes 5242880 | tf_op jit(solution)/shard_map/all_gather | solution.py:187
  567.8 92.6 %collective-permute-start.25 = (bf16[4,16,128,256]{3,2,1,0:T(8,128)(2,1)}, bf16[4,16,128,256]{3,2,1,0:T(8,128)(2,1)}, u32[]{:S(2)}, u32[]{:S(2)}) collective-permute-start(bf16[4,16,128,256]{3,2,1,0:T(8,128)(2,1)} %all-gather.9.cloned.1.call-done.refs_5_.refs_2_), channel_id=1, source_target_pairs={{0,1},{1,0},{2,3},{3,2},{4,5},{5,4},{6,7},{7,6},{8,9},{9,8},{10,11... | collective-permute-start | bytes 12582920 | tf_op jit(solution)/shard_map/ppermute | solution.py:31
  571.4 102.0 %collective-permute-start.26 = (bf16[16,128,256]{2,1,0:T(8,128)(2,1)S(1)}, bf16[16,128,256]{2,1,0:T(8,128)(2,1)S(1)}, u32[]{:S(2)}, u32[]{:S(2)}) collective-permute-start(bf16[16,128,256]{2,1,0:T(8,128)(2,1)S(1)} %convolution_convert_fusion), channel_id=1, source_target_pairs={{0,1},{1,0},{8,9},{9,8},{16,17},{17,16},{24,25},{25,24}} | collective-permute-start | bytes 3145736 | tf_op jit(solution)/shard_map/ppermute | solution.py:31
  678.5 260.2 %all-gather.15.cloned.1.call-start = ((), (), s32[]{:S(2)}) async-start(), calls=%async_computation.3 | async-start | bytes 5242880 | tf_op jit(solution)/shard_map/all_gather | solution.py:187
  679.2 93.0 %collective-permute-start.28 = (bf16[4,16,128,256]{3,2,1,0:T(8,128)(2,1)}, bf16[4,16,128,256]{3,2,1,0:T(8,128)(2,1)}, u32[]{:S(2)}, u32[]{:S(2)}) collective-permute-start(bf16[4,16,128,256]{3,2,1,0:T(8,128)(2,1)} %all-gather.11.cloned.1.call-done.refs_5_.refs_2_), channel_id=1, source_target_pairs={{0,1},{1,0},{2,3},{3,2},{4,5},{5,4},{6,7},{7,6},{8,9},{9,8},{10,11... | collective-permute-start | bytes 12582920 | tf_op jit(solution)/shard_map/ppermute | solution.py:31
  680.5 181.7 %collective-permute-start.29 = (bf16[4,16,128,256]{3,2,1,0:T(8,128)(2,1)}, bf16[4,16,128,256]{3,2,1,0:T(8,128)(2,1)}, u32[]{:S(2)}, u32[]{:S(2)}) collective-permute-start(bf16[4,16,128,256]{3,2,1,0:T(8,128)(2,1)} %all-gather.23.cloned.1.call-done.refs_3_), channel_id=1, source_target_pairs={{0,1},{1,0},{2,3},{3,2},{4,5},{5,4},{6,7},{7,6},{8,9},{9,8},{10,11... | collective-permute-start | bytes 12582920 | tf_op jit(solution)/shard_map/ppermute | solution.py:31
  680.8 257.9 %collective-permute-start.27 = (bf16[4,16,128,256]{3,2,1,0:T(8,128)(2,1)}, bf16[4,16,128,256]{3,2,1,0:T(8,128)(2,1)}, u32[]{:S(2)}, u32[]{:S(2)}) collective-permute-start(bf16[4,16,128,256]{3,2,1,0:T(8,128)(2,1)} %all-gather.13.cloned.1.call-done.refs_5_.refs_3_), channel_id=1, source_target_pairs={{0,1},{1,0},{2,3},{3,2},{4,5},{5,4},{6,7},{7,6},{8,9},{9,8},{10,11... | collective-permute-start | bytes 12582920 | tf_op jit(solution)/shard_map/ppermute | solution.py:31
  (53 other events, 822.7 us)
Sparse Core Ops, SparseCore 0:
  250.1 83.2 all-gather.8
  334.9 79.6 all-gather.10
  416.2 78.9 all-gather.12
  496.6 79.2 all-gather.22
  577.3 79.2 all-gather.20
  658.1 79.2 all-gather.18
  739.5 79.2 all-gather.16
  820.4 79.2 all-gather.14
